TPU v7x, 32 devices: a whole 2x2x4 slice. The times are simulated.
32 devices in a mesh: pas: 16 (over z, y, core), tp: 2 (over x).
Axes of the slice: x: 2, y: 2, z: 4, core: 2. Of those that a mesh axis runs over, the one named last changes fastest.
Arguments:
- passage_hidden: bfloat16 [16384, 8192], P('pas', 'tp'), may hold values from -6 to 6
- kv_weight: bfloat16 [1024, 8192], P('pas', 'tp'), may hold values from -0.0625 to 0.0625
- queries: bfloat16 [8192, 4096], P('pas', 'tp'), may hold values from -600 to 600
- query_kv: bfloat16 [8192, 1024], P('pas', 'tp'), may hold values from -6 to 6
- out_grad: bfloat16 [8192, 4096], P('pas', 'tp'), may hold values from -6 to 6
- source_device: int32 [64, 8], P('pas'), may hold values from 0 to 15, all different within a row; in each aligned block of 4 rows (0 to 3, 4 to 7, ...) at most 4 rows name the same one
- source_slot: int32 [64, 8], P('pas'), may hold values from 0 to 7
Outputs:
- query_grad: bfloat16 [8192, 4096], P('pas', 'tp')
- query_kv_grad: bfloat16 [8192, 1024], P('pas', 'tp')
- weight_grad: float32 [1024, 8192], P('pas', 'tp')
Inputs may be any that keep to these rules, and one draw needn't show every extreme that they name: `source_device`: each query names 8 different owners; among the 4 queries of one index of pas no owner is named more than 4 times, and one owner exactly 4 times.
All inputs are finite; a program needn't handle non-finite values.
Results may differ from a plain program's by a relative error of at most 0.0095.
Values may be sent and summed in bfloat16 or wider, within the bound.
A program may use at most 128 MiB of HBM per device.

v0:
```python
import jax
import jax.numpy as jnp
from jax import lax
from jax.sharding import PartitionSpec as P

HD = 128
PLEN = 128


def attend_block(query_rows, keys_values, grad_out, prefix):
    query_len = query_rows.shape[0]
    key_len = keys_values.shape[0]
    kv_heads = keys_values.shape[1] // (2 * HD)
    group_size = query_rows.shape[1] // (HD * kv_heads)
    paired = keys_values.reshape(key_len, kv_heads, 2, HD)
    key_heads = paired[:, :, 0, :]
    value_heads = paired[:, :, 1, :]
    query_heads = query_rows.reshape(query_len, kv_heads, group_size, HD)
    grad_heads = grad_out.reshape(query_len, kv_heads, group_size, HD)
    scaling = HD ** (-0.5)
    scores = (
        jnp.einsum("qhgd,khd->hgqk", query_heads, key_heads, preferred_element_type=jnp.float32)
        * scaling
    )
    row_index = jnp.arange(query_len)[:, None]
    col_index = jnp.arange(key_len)[None, :]
    visible = jnp.logical_or(col_index < prefix, col_index - prefix <= row_index)
    scores = jnp.where(visible, scores, jnp.float32(-1e30))
    largest = jnp.max(scores, axis=-1, keepdims=True)
    exponent = jnp.exp(scores - largest)
    weights = exponent / jnp.sum(exponent, axis=-1, keepdims=True)
    weights_low = weights.astype(jnp.bfloat16)
    outputs = jnp.einsum(
        "hgqk,khd->hgqd", weights_low, value_heads, preferred_element_type=jnp.float32
    )
    grad_float = grad_heads.astype(jnp.float32).transpose(1, 2, 0, 3)
    delta_rows = jnp.sum(outputs * grad_float, axis=-1, keepdims=True)
    grad_weights = jnp.einsum(
        "qhgd,khd->hgqk", grad_heads, value_heads, preferred_element_type=jnp.float32
    )
    grad_low = (weights * (grad_weights - delta_rows)).astype(jnp.bfloat16)
    grad_query = (
        jnp.einsum("hgqk,khd->qhgd", grad_low, key_heads, preferred_element_type=jnp.float32)
        * scaling
    )
    grad_query = grad_query.astype(jnp.bfloat16).reshape(query_len, kv_heads * group_size * HD)
    grad_keys = (
        jnp.einsum("hgqk,qhgd->khd", grad_low, query_heads, preferred_element_type=jnp.float32)
        * scaling
    )
    grad_values = jnp.einsum(
        "hgqk,qhgd->khd", weights_low, grad_heads, preferred_element_type=jnp.float32
    )
    grad_pairs = jnp.stack([grad_keys, grad_values], axis=2).reshape(key_len, kv_heads * 2 * HD)
    return (grad_query, grad_pairs)


def per_device(passage_hidden, kv_weight, queries, query_kv, out_grad, source_device, source_slot):
    owners = lax.axis_size("pas")
    rows_local = passage_hidden.shape[0]
    local_width = query_kv.shape[1]
    passages_here = rows_local // PLEN
    queries_here = source_device.shape[0]
    retrieved = source_device.shape[1]
    requests_total = queries_here * retrieved
    capacity = min(queries_here, max(2, 2 * requests_total // owners))
    query_length = queries.shape[0] // queries_here
    partial_kv = jnp.einsum(
        "rd,cd->rc",
        passage_hidden,
        lax.all_gather(kv_weight, "pas", axis=0, tiled=True),
        preferred_element_type=jnp.float32,
    )
    passage_kv = lax.psum_scatter(partial_kv, "tp", scatter_dimension=1, tiled=True).astype(
        jnp.bfloat16
    )
    passage_kv = passage_kv.reshape(passages_here, PLEN, local_width)
    flat_device = source_device.reshape(-1)
    flat_slot = source_slot.reshape(-1)
    owner_hits = (flat_device[:, None] == jnp.arange(owners, dtype=jnp.int32)[None, :]).astype(
        jnp.int32
    )
    earlier = jnp.cumsum(owner_hits, axis=0) - owner_hits
    ranking = jnp.sum(owner_hits * earlier, axis=1)
    slot_hits = (ranking[:, None] == jnp.arange(capacity, dtype=jnp.int32)[None, :]).astype(
        jnp.int32
    )
    placed = owner_hits[:, :, None] * slot_hits[:, None, :]
    request_table = jnp.sum(placed * (flat_slot + 1)[:, None, None], axis=0) - 1
    wanted = lax.all_to_all(request_table, "pas", split_axis=0, concat_axis=0, tiled=True)
    global_ids = flat_device * passages_here + flat_slot
    initial = jnp.zeros((requests_total, PLEN, local_width), jnp.bfloat16)
    piece_rows = lax.all_gather(passage_kv, "pas", axis=0, tiled=True)
    inside = jnp.logical_and(global_ids >= 0, global_ids < piece_rows.shape[0])
    taken_rows = piece_rows[jnp.clip(global_ids, 0, piece_rows.shape[0] - 1)]
    fetched = jnp.where(inside[:, None, None], taken_rows, initial)
    remote_rows = retrieved * PLEN

    def one_query(inputs):
        query_rows, own_pairs, grad_out, remote_pairs = inputs
        keys_values = jnp.concatenate([remote_pairs, own_pairs], axis=0)
        grad_query, grad_pairs = attend_block(query_rows, keys_values, grad_out, remote_rows)
        return (
            grad_query,
            grad_pairs[:remote_rows].astype(jnp.bfloat16),
            grad_pairs[remote_rows:].astype(jnp.bfloat16),
        )

    grad_queries, remote_grads, own_grads = lax.map(
        one_query,
        (
            queries.reshape(queries_here, query_length, queries.shape[1]),
            query_kv.reshape(queries_here, query_length, local_width),
            out_grad.reshape(queries_here, query_length, out_grad.shape[1]),
            fetched.reshape(queries_here, remote_rows, local_width),
        ),
    )
    outgoing_grads = jnp.zeros((owners, capacity, PLEN, local_width), jnp.bfloat16)
    outgoing_grads = outgoing_grads.at[flat_device, ranking].set(
        remote_grads.reshape(requests_total, PLEN, local_width)
    )
    returned = lax.all_to_all(outgoing_grads, "pas", split_axis=0, concat_axis=0, tiled=True)
    slot_select = (
        wanted[:, :, None] == jnp.arange(passages_here, dtype=jnp.int32)[None, None, :]
    ).astype(jnp.bfloat16)
    grad_total = jnp.einsum(
        "ncs,ncpk->spk", slot_select, returned, preferred_element_type=jnp.float32
    )
    grad_kv = grad_total.astype(jnp.bfloat16).reshape(rows_local, local_width)
    full_grad = lax.all_gather(grad_kv, "tp", axis=1, tiled=True)
    weight_grad = lax.psum_scatter(
        jnp.einsum("rc,rd->cd", full_grad, passage_hidden, preferred_element_type=jnp.float32),
        "pas",
        scatter_dimension=0,
        tiled=True,
    )
    return (
        grad_queries.reshape(queries_here * query_length, queries.shape[1]),
        own_grads.reshape(queries_here * query_length, local_width),
        weight_grad,
    )


def solution(mesh):
    in_specs = (
        P("pas", "tp"),
        P("pas", "tp"),
        P("pas", "tp"),
        P("pas", "tp"),
        P("pas", "tp"),
        P("pas", None),
        P("pas", None),
    )
    out_specs = (P("pas", "tp"), P("pas", "tp"), P("pas", "tp"))
    return jax.shard_map(
        per_device, mesh=mesh, in_specs=in_specs, out_specs=out_specs, check_vma=False
    )
```

profile of v0, /device:TPU:0, one launch (start us, length us, event | category | flops | bytes accessed | tf_op | source)
XLA Modules:
  0.0 867.9 jit_solution(764255329276015901)
XLA Ops:
  7.9 79.8 %all-gather.4.cloned.1.call-done = bf16[1024,4096]{1,0:T(8,128)(2,1)} async-done(((bf16[64,4096]{1,0:T(8,128)(2,1)}), bf16[1024,4096]{1,0:T(8,128)(2,1)}) %all-gather.4.cloned.1.call-update) | async-done | bytes 8388624 | tf_op jit(solution)/shard_map/all_gather | solution.py:71
  87.8 15.1 %fusion.43 = f32[1024,1024]{1,0:T(8,128)} fusion(bf16[1024,4096]{1,0:T(8,128)(2,1)} %param.9, bf16[1024,4096]{1,0:T(8,128)(2,1)} %all-gather.4.cloned.1.call-done), kind=kOutput, calls=%fused_computation.76 | convolution fusion | flops 8589934592 | bytes 20971520 | tf_op jit(solution)/shard_map/rd,cd->rc/dot_general | solution.py:68
  102.9 52.7 %reduce-scatter.3.cloned.1.call-done = f32[1024,512]{1,0:T(8,128)} async-done(((f32[1024,1024]{1,0:T(8,128)}), f32[1024,512]{1,0:T(8,128)}) %reduce-scatter.3.cloned.1.call-update) | async-done | bytes 2097168 | tf_op jit(solution)/shard_map/reduce_scatter | solution.py:74
  155.6 2.7 convert_element_type.74
  159.8 5.7 all-to-all-start
  166.3 119.1 %all-gather.6.cloned.1.call-done = bf16[128,128,512]{2,1,0:T(8,128)(2,1)} async-done(((bf16[8,128,512]{2,1,0:T(8,128)(2,1)}), bf16[128,128,512]{2,1,0:T(8,128)(2,1)}) %all-gather.6.cloned.1.call-update) | async-done | bytes 16777232 | tf_op jit(solution)/shard_map/all_gather | solution.py:93
  285.4 8.5 gather_fusion
  294.0 4.0 bitcast_select_fusion.2
  297.9 112.0 %while.17 = (s32[]{:T(128)}, bf16[4,128,2048]{2,1,0:T(8,128)(2,1)}, bf16[4,1024,512]{2,1,0:T(8,128)(2,1)}, bf16[4,128,512]{2,1,0:T(8,128)(2,1)}, bf16[4,1024,512...) while((s32[]{:T(128)}, bf16[4,128,2048]{2,1,0:T(8,128)(2,1)}, ...), condition=%wide.region_5.6_spmd.clone, body=%wide.region_1.5_spmd.sunk.clone | while | flops 3655239168 | bytes 129977736 | solution.py:109
  300.0 1.3 constant_dynamic-slice_fusion.11
  302.5 1.3 constant_dynamic-slice_fusion.10
  304.4 5.5 fusion.108
  309.8 5.0 fusion.109
  316.2 1.8 fusion.111
  318.0 1.6 convolution_bitcast_fusion.4
  320.5 1.6 fusion.113
  328.0 1.3 constant_dynamic-slice_fusion.11
  330.5 1.3 constant_dynamic-slice_fusion.10
  332.4 5.5 fusion.108
  337.8 5.0 fusion.109
  344.2 1.8 fusion.111
  346.0 1.6 convolution_bitcast_fusion.4
  348.5 1.6 fusion.113
  352.9 1.1 constant_dynamic-update-slice_fusion.10
  356.0 1.3 constant_dynamic-slice_fusion.11
  358.6 1.3 constant_dynamic-slice_fusion.10
  360.4 5.5 fusion.108
  365.9 5.0 fusion.109
  372.2 1.8 fusion.111
  374.0 1.6 convolution_bitcast_fusion.4
  376.5 1.6 fusion.113
  384.0 1.3 constant_dynamic-slice_fusion.11
  386.6 1.3 constant_dynamic-slice_fusion.10
  388.4 5.5 fusion.108
  393.9 5.0 fusion.109
  400.2 1.8 fusion.111
  402.0 1.6 convolution_bitcast_fusion.4
  404.5 1.6 fusion.113
  410.0 4.2 broadcast_in_dim.73
  414.2 11.6 %scatter_fusion = bf16[16,4,128,512]{3,2,1,0:T(8,128)(2,1)} fusion(bf16[16,4,128,512]{3,2,1,0:T(8,128)(2,1)} %broadcast_in_dim.73, s32[32]{0:T(128)S(1)} %copy-done.1, bf16[32,128,512]{2,1,0:T(8,128)(2,1)} %bitcast.201), kind=kCustom, calls=%fused_computation.1 | custom fusion | bytes 12583168 | tf_op jit(solution)/shard_map/scatter | solution.py:119
  425.8 11.0 %copy.107 = bf16[16,4,128,512]{3,1,2,0:T(4,128)(2,1)} copy(bf16[16,4,128,512]{3,2,1,0:T(8,128)(2,1)} %scatter_fusion) | data formatting | bytes 16777216 | tf_op jit(solution)/shard_map/scatter | solution.py:119
  436.8 4.8 all-to-all-start.1
  442.4 149.8 %all-to-all-done.1 = bf16[16,4,128,512]{3,1,2,0:T(4,128)(2,1)} async-done(((bf16[16,4,128,512]{3,1,2,0:T(4,128)(2,1)}), bf16[16,4,128,512]{3,1,2,0:T(4,128)(2,1)}, u32[]{:S(2)}, u32[]{:S(2)}) %all-to-all-start.1) | async-done | bytes 8388640 | tf_op jit(solution)/shard_map/all_to_all | solution.py:122
  592.2 7.9 bitcast_convert_fusion
  600.2 1.3 copy.109
  601.5 65.0 %all-gather.8.cloned.1.call-done = bf16[1024,1024]{1,0:T(8,128)(2,1)} async-done(((bf16[1024,512]{1,0:T(8,128)(2,1)}), bf16[1024,1024]{1,0:T(8,128)(2,1)}) %all-gather.8.cloned.1.call-update) | async-done | bytes 2097168 | tf_op jit(solution)/shard_map/all_gather | solution.py:130
  666.5 16.1 %fusion.44 = f32[1024,4096]{1,0:T(8,128)} fusion(bf16[1024,1024]{1,0:T(8,128)(2,1)} %all-gather.8.cloned.1.call-done, bf16[1024,4096]{1,0:T(8,128)(2,1)} %param.9), kind=kOutput, calls=%fused_computation.77 | convolution fusion | flops 8589934592 | bytes 27262976 | tf_op jit(solution)/shard_map/rc,rd->cd/dot_general | solution.py:132
  682.7 178.7 %reduce-scatter.5.cloned.1.call-done = f32[64,4096]{1,0:T(8,128)} async-done(((f32[1024,4096]{1,0:T(8,128)}), f32[64,4096]{1,0:T(8,128)}) %reduce-scatter.5.cloned.1.call-update) | async-done | bytes 1048592 | tf_op jit(solution)/shard_map/reduce_scatter | solution.py:131
  (138 shorter events, 42.5 us)
Async XLA Ops:
  7.2 80.6 %all-gather.4.cloned.1.call-start = ((), (), s32[]{:S(2)}) async-start(), calls=%async_computation.4 | async-start | bytes 8912896 | tf_op jit(solution)/shard_map/all_gather | solution.py:71
  7.9 147.7 %reduce-scatter.3.cloned.1.call-start = ((), (), s32[]{:S(2)}) async-start(), calls=%async_computation.5 | async-start | bytes 6291456 | tf_op jit(solution)/shard_map/reduce_scatter | solution.py:74
  102.9 55.5 %copy-start.3 = (s32[4,8]{1,0:T(4,128)S(1)}, s32[4,8]{1,0:T(4,128)}, u32[]{:S(2)}) copy-start(s32[4,8]{1,0:T(4,128)} %param.14) | copy-start | bytes 388
  102.9 55.6 %copy-start.2 = (s32[4,8]{1,0:T(4,128)S(1)}, s32[4,8]{1,0:T(4,128)}, u32[]{:S(2)}) copy-start(s32[4,8]{1,0:T(4,128)} %param.15) | copy-start | bytes 388
  102.9 182.5 %all-gather.6.cloned.1.call-start = ((), (), s32[]{:S(2)}) async-start(), calls=%async_computation.6 | async-start | bytes 17825792 | tf_op jit(solution)/shard_map/all_gather | solution.py:93
  159.8 277.1 %all-to-all-start = ((s32[16,1,4]{2,1,0:T(1,128)}), s32[16,1,4]{2,1,0:T(1,128)}, u32[]{:S(2)}, u32[]{:S(2)}) async-start(s32[16,1,4]{2,1,0:T(1,128)} %copy.104), calls=%async_computation.1 | async-start | bytes 16384 | tf_op jit(solution)/shard_map/all_to_all | solution.py:90
  309.8 6.4 copy-start
  337.8 6.4 copy-start
  365.9 6.4 copy-start
  393.9 6.4 copy-start
  410.0 4.2 copy-start.1
  436.8 155.4 %all-to-all-start.1 = ((bf16[16,4,128,512]{3,1,2,0:T(4,128)(2,1)}), bf16[16,4,128,512]{3,1,2,0:T(4,128)(2,1)}, u32[]{:S(2)}, u32[]{:S(2)}) async-start(bf16[16,4,128,512]{3,1,2,0:T(4,128)(2,1)} %copy.107), calls=%async_computation.2 | async-start | bytes 16777216 | tf_op jit(solution)/shard_map/all_to_all | solution.py:122
  441.6 224.9 %all-gather.8.cloned.1.call-start = ((), (), s32[]{:S(2)}) async-start(), calls=%async_computation.7 | async-start | bytes 3145728 | tf_op jit(solution)/shard_map/all_gather | solution.py:130
  601.5 259.9 %reduce-scatter.5.cloned.1.call-start = ((), (), s32[]{:S(2)}) async-start(), calls=%async_computation.8 | async-start | bytes 17825792 | tf_op jit(solution)/shard_map/reduce_scatter | solution.py:131
Sparse Core Ops, SparseCore 0:
  10.2 77.5 all-gather.3
  103.0 52.5 reduce-scatter.2
  158.6 126.7 all-gather.5
  601.6 64.8 all-gather.7
  682.8 178.5 reduce-scatter.4
where the time goes:
time: 869 us; the launch traced here: 868 us
  waiting for transfers between devices  646 us (74%)
  matrix products  88.3 us (10%)
  local copies, waits for them, and re-layouts  76.8 us (9%)
  other arithmetic  31.7 us (4%)
  between operations  13.8 us (2%)
  starting transfers between devices  10.7 us (1%)
    reduce_scatter x1, waiting for transfers between devices, per_device(): lax.psum_scatter(jnp.einsum('rc,rd->cd', full_grad, passage_hidden, prefe...  179 us
    all_to_all x1, waiting for transfers between devices, per_device(): lax.all_to_all(outgoing_grads, 'pas', split_axis=0, concat_axis=0, tiled=...  150 us
    all_gather x1, waiting for transfers between devices, per_device(): piece_rows = lax.all_gather(passage_kv, 'pas', axis=0, tiled=True)  119 us
    all_gather x1, waiting for transfers between devices, per_device(): lax.all_gather(kv_weight, 'pas', axis=0, tiled=True)  79.8 us
    all_gather x1, waiting for transfers between devices, per_device(): full_grad = lax.all_gather(grad_kv, 'tp', axis=1, tiled=True)  65 us
    reduce_scatter x1, waiting for transfers between devices, per_device(): lax.psum_scatter(partial_kv, 'tp', scatter_dimension=1, tiled=True)  52.7 us
    scatter x2, local copies, waits for them, and re-layouts, per_device(): outgoing_grads.at[flat_device, ranking]  22.6 us
    sub x4, matrix products, attend_block(): exponent = jnp.exp(scores - largest)  21.9 us
  transfers between devices with their start and end apart: 7, of which 6 were waited for; matrix products, arithmetic and copies ran while one was open for 18% of the time, Pallas kernels for 0%

commit v1 on v0

v1 whole, which is shorter than its diff:
```python
import functools
import math
import jax
import jax.numpy as jnp
from jax import lax
from jax.experimental import pallas as pl
from jax.experimental.pallas import tpu as pltpu
from jax.sharding import PartitionSpec as P

HD = 128
PLEN = 128
MIB = 1 << 20


def ring_place(chips):
    me = lax.axis_index("pas")
    core = lax.rem(me, 2)
    chip = lax.div(me, 2)
    side = lax.rem(chip, 2)
    deep = lax.div(chip, 2)
    place = deep + side * (chips - 1 - 2 * deep)

    def chip_at(position):
        q = lax.rem(position + 2 * chips, chips)
        half = lax.div(q, chips // 2)
        return 2 * q + half * (2 * chips - 1 - 4 * q)

    return core, place, chip_at


def greet(others):
    barrier = pltpu.get_barrier_semaphore()
    for other in others:
        pl.semaphore_signal(
            barrier, inc=1, device_id={"pas": other}, device_id_type=pl.DeviceIdType.MESH
        )
    pl.semaphore_wait(barrier, len(others))


def send(src, dst, send_sem, recv_sem, other):
    return pltpu.make_async_remote_copy(
        src_ref=src,
        dst_ref=dst,
        send_sem=send_sem,
        recv_sem=recv_sem,
        device_id={"pas": other},
        device_id_type=pl.DeviceIdType.MESH,
    )


def gather_kernel(chips, lanes, x_ref, out_ref, own_sem, ring_send, ring_recv, pair_send, pair_recv):
    core, place, chip_at = ring_place(chips)
    mine = chip_at(place)
    partner = 2 * mine + 1 - core
    nexts = (2 * chip_at(place + 1) + core, 2 * chip_at(place - 1) + core)
    greet((nexts[0], nexts[1], partner))
    rings, pairs = {}, []
    for step in range(chips):
        for lane in range(lanes):
            for way in range(2):
                back = step if way == 0 else -step
                where = chip_at(place - back)
                slot = out_ref.at[where, core, way, lane]
                if step == 0:
                    src = x_ref.at[way, lane]
                else:
                    rings[step - 1, way, lane].wait_recv()
                    src = slot
                if step < chips - 1:
                    copy = send(
                        src, slot, ring_send.at[step, way, lane], ring_recv.at[step, way, lane], nexts[way]
                    )
                    copy.start()
                    rings[step, way, lane] = copy
                copy = send(
                    src, slot, pair_send.at[step, way, lane], pair_recv.at[step, way, lane], partner
                )
                copy.start()
                pairs.append(copy)
        if step == 0:
            own = pltpu.make_async_copy(x_ref, out_ref.at[mine, core], own_sem)
            own.start()
    own.wait()
    for copy in rings.values():
        copy.wait_send()
    for copy in pairs:
        copy.wait()


def ring_gather(x, chips, collective_id):
    rows, width = x.shape
    lanes = 2 if rows % 64 == 0 else 1
    high = rows // (2 * lanes)
    out = pl.pallas_call(
        functools.partial(gather_kernel, chips, lanes),
        out_shape=jax.ShapeDtypeStruct((chips, 2, 2, lanes, high, width), x.dtype),
        in_specs=[pl.BlockSpec(memory_space=pl.ANY)],
        out_specs=pl.BlockSpec(memory_space=pl.ANY),
        scratch_shapes=[
            pltpu.SemaphoreType.DMA,
            pltpu.SemaphoreType.DMA((chips, 2, lanes)),
            pltpu.SemaphoreType.DMA((chips, 2, lanes)),
            pltpu.SemaphoreType.DMA((chips, 2, lanes)),
            pltpu.SemaphoreType.DMA((chips, 2, lanes)),
        ],
        compiler_params=pltpu.CompilerParams(collective_id=collective_id, has_side_effects=True),
    )(x.reshape(2, lanes, high, width))
    return out.reshape(chips * 2 * rows, width)


def sum_kernel(
    chips, lanes, x_ref, out_ref, mine, pair, got,
    own_sem, pair_send, pair_recv, ring_send, ring_recv,
):
    core, place, chip_at = ring_place(chips)
    partner = 2 * chip_at(place) + 1 - core
    nexts = (2 * chip_at(place + 1) + core, 2 * chip_at(place - 1) + core)
    high = x_ref.shape[4]
    part = 16
    owns, pairs, rings = {}, {}, {}
    greet((nexts[0], nexts[1], partner))
    for step in range(chips):
        for way in range(2):
            ahead = place - 1 - step if way == 0 else place + 1 + step
            where = chip_at(ahead)
            copy = send(
                x_ref.at[where, 1 - core, way],
                pair.at[way, step],
                pair_send.at[way, step],
                pair_recv.at[way, step],
                partner,
            )
            copy.start()
            pairs[way, step] = copy
            copy = pltpu.make_async_copy(
                x_ref.at[where, core, way], mine.at[way, step], own_sem.at[way, step]
            )
            copy.start()
            owns[way, step] = copy
    for step in range(chips):
        last = step == chips - 1
        for lane in range(lanes):
            for way in range(2):
                if lane == 0:
                    owns[way, step].wait()
                    pairs[way, step].wait_recv()
                if step > 0:
                    rings[step - 1, way, lane].wait_recv()

                def add(index, carry, way=way, lane=lane):
                    here = pl.ds(pl.multiple_of(index * part, part), part)
                    total = mine[way, step, lane, here, :].astype(jnp.float32)
                    total += pair[way, step, lane, here, :].astype(jnp.float32)
                    if step > 0:
                        total += got[way, step - 1, lane, here, :].astype(jnp.float32)
                    if last:
                        out_ref[way, lane, here, :] = total.astype(out_ref.dtype)
                    else:
                        mine[way, step, lane, here, :] = total.astype(mine.dtype)
                    return carry

                lax.fori_loop(0, high // part, add, 0)
                if not last:
                    copy = send(
                        mine.at[way, step, lane],
                        got.at[way, step, lane],
                        ring_send.at[step, way, lane],
                        ring_recv.at[step, way, lane],
                        nexts[way],
                    )
                    copy.start()
                    rings[step, way, lane] = copy
    for copy in pairs.values():
        copy.wait_send()
    for copy in rings.values():
        copy.wait_send()


def ring_sum(x, chips, collective_id, out_dtype):
    rows, width = x.shape
    rows = rows // (2 * chips)
    lanes = 2 if rows % 64 == 0 else 1
    high = rows // (2 * lanes)
    block = (lanes, high, width)
    out = pl.pallas_call(
        functools.partial(sum_kernel, chips, lanes),
        out_shape=jax.ShapeDtypeStruct((2,) + block, out_dtype),
        in_specs=[pl.BlockSpec(memory_space=pl.ANY)],
        out_specs=pl.BlockSpec(memory_space=pltpu.VMEM),
        scratch_shapes=[
            pltpu.VMEM((2, chips) + block, x.dtype),
            pltpu.VMEM((2, chips) + block, x.dtype),
            pltpu.VMEM((2, chips) + block, x.dtype),
            pltpu.SemaphoreType.DMA((2, chips)),
            pltpu.SemaphoreType.DMA((2, chips)),
            pltpu.SemaphoreType.DMA((2, chips)),
            pltpu.SemaphoreType.DMA((chips, 2, lanes)),
            pltpu.SemaphoreType.DMA((chips, 2, lanes)),
        ],
        compiler_params=pltpu.CompilerParams(
            collective_id=collective_id, has_side_effects=True, vmem_limit_bytes=48 * MIB
        ),
    )(x.reshape((chips, 2, 2) + block))
    return out.reshape(rows, width)


def attend_kernel(group, retrieved, ids_ref, q_ref, g_ref, own_ref, *refs):
    passages = refs[:retrieved]
    dq_ref, remote_ref, down_ref, keys, values, dkeys, dvalues = refs[retrieved:]
    scaling = HD ** (-0.5)
    remote = retrieved * PLEN
    tokens = q_ref.shape[0]
    for i in range(retrieved):
        keys[i * PLEN : (i + 1) * PLEN, :] = passages[i][0, :, :HD]
        values[i * PLEN : (i + 1) * PLEN, :] = passages[i][0, :, HD:]
    keys[remote:, :] = own_ref[:, :HD]
    values[remote:, :] = own_ref[:, HD:]
    row = lax.broadcasted_iota(jnp.int32, (2 * tokens, tokens), 0)
    col = lax.broadcasted_iota(jnp.int32, (2 * tokens, tokens), 1)
    hidden = col > jnp.where(row >= tokens, row - tokens, row)

    def dot(a, b, dims):
        return lax.dot_general(a, b, ((dims[0], dims[1]), ((), ())), preferred_element_type=jnp.float32)

    for pair in range(group // 2):
        lo, mid, hi = 2 * pair * HD, (2 * pair + 1) * HD, (2 * pair + 2) * HD
        q = jnp.concatenate([q_ref[:, lo:mid], q_ref[:, mid:hi]], axis=0)
        g = jnp.concatenate([g_ref[:, lo:mid], g_ref[:, mid:hi]], axis=0)
        k, v = keys[...], values[...]
        scores = dot(q, k, ((1,), (1,)))
        tail = jnp.where(hidden, jnp.float32(-1e30), scores[:, remote:])
        scores = jnp.concatenate([scores[:, :remote], tail], axis=1)
        largest = jnp.max(scores, axis=1, keepdims=True)
        exponent = jnp.exp2((scores - largest) * jnp.float32(scaling * math.log2(math.e)))
        weights = exponent * (1.0 / jnp.sum(exponent, axis=1, keepdims=True))
        low = weights.astype(jnp.bfloat16)
        outputs = dot(low, v, ((1,), (0,)))
        delta = jnp.sum(outputs * g.astype(jnp.float32), axis=1, keepdims=True)
        grad = (weights * (dot(g, v, ((1,), (1,))) - delta)).astype(jnp.bfloat16)
        dq = (dot(grad, k, ((1,), (0,))) * scaling).astype(dq_ref.dtype)
        dq_ref[:, lo:mid] = dq[:tokens]
        dq_ref[:, mid:hi] = dq[tokens:]
        dk = dot(grad, q, ((0,), (0,)))
        dv = dot(low, g, ((0,), (0,)))
        if pair == 0:
            dkeys[...] = dk
            dvalues[...] = dv
        else:
            dkeys[...] += dk
            dvalues[...] += dv
    for i in range(retrieved):
        remote_ref[i, :, :HD] = (dkeys[i * PLEN : (i + 1) * PLEN, :] * scaling).astype(remote_ref.dtype)
        remote_ref[i, :, HD:] = dvalues[i * PLEN : (i + 1) * PLEN, :].astype(remote_ref.dtype)
    down_ref[:, :HD] = (dkeys[remote:, :] * scaling).astype(down_ref.dtype)
    down_ref[:, HD:] = dvalues[remote:, :].astype(down_ref.dtype)


def attend(ids, queries, out_grad, query_kv, passage_kv, queries_here, retrieved):
    tokens = queries.shape[0] // queries_here
    width = query_kv.shape[1]
    heads = width // (2 * HD)
    wide = queries.shape[1] // heads
    group = wide // HD
    keys = retrieved * PLEN + tokens

    def passage_spec(i):
        return pl.BlockSpec((1, PLEN, 2 * HD), lambda n, h, ids: (ids[n * retrieved + i], 0, h))

    wide_spec = pl.BlockSpec((tokens, wide), lambda n, h, ids: (n, h))
    own_spec = pl.BlockSpec((tokens, 2 * HD), lambda n, h, ids: (n, h))
    flops = 12 * queries_here * heads * group * tokens * keys * HD
    return pl.pallas_call(
        functools.partial(attend_kernel, group, retrieved),
        grid_spec=pltpu.PrefetchScalarGridSpec(
            num_scalar_prefetch=1,
            grid=(queries_here, heads),
            in_specs=[wide_spec, wide_spec, own_spec] + [passage_spec(i) for i in range(retrieved)],
            out_specs=[
                wide_spec,
                pl.BlockSpec((retrieved, PLEN, 2 * HD), lambda n, h, ids: (n, 0, h)),
                own_spec,
            ],
            scratch_shapes=[
                pltpu.VMEM((keys, HD), jnp.bfloat16),
                pltpu.VMEM((keys, HD), jnp.bfloat16),
                pltpu.VMEM((keys, HD), jnp.float32),
                pltpu.VMEM((keys, HD), jnp.float32),
            ],
        ),
        out_shape=[
            jax.ShapeDtypeStruct(queries.shape, jnp.bfloat16),
            jax.ShapeDtypeStruct((queries_here * retrieved, PLEN, width), jnp.bfloat16),
            jax.ShapeDtypeStruct(query_kv.shape, jnp.bfloat16),
        ],
        compiler_params=pltpu.CompilerParams(vmem_limit_bytes=48 * MIB),
        cost_estimate=pl.CostEstimate(flops=flops, bytes_accessed=16 * MIB, transcendentals=0),
    )(ids, queries, out_grad, query_kv, *([passage_kv] * retrieved))


def per_device(passage_hidden, kv_weight, queries, query_kv, out_grad, source_device, source_slot):
    owners = lax.axis_size("pas")
    shares = lax.axis_size("tp")
    share = lax.axis_index("tp")
    chips = owners // 2
    rows_local = passage_hidden.shape[0]
    local_width = query_kv.shape[1]
    passages_here = rows_local // PLEN
    queries_here, retrieved = source_device.shape
    weight = ring_gather(kv_weight, chips, 0)

    def project(target):
        rows = lax.dynamic_slice_in_dim(weight, target * local_width, local_width, axis=0)
        return lax.dot_general(
            passage_hidden, rows, (((1,), (1,)), ((), ())), preferred_element_type=jnp.float32
        )

    arrived = []
    for k in range(1, shares):
        route = [(i, (i + k) % shares) for i in range(shares)]
        arrived.append(lax.ppermute(project(lax.rem(share + k, shares)), "tp", route))
    projected = project(share)
    for block in arrived:
        projected = projected + block
    passage_kv = ring_gather(projected.astype(jnp.bfloat16), chips, 1)
    passage_kv = passage_kv.reshape(owners * passages_here, PLEN, local_width)
    ids = (source_device * passages_here + source_slot).reshape(-1)
    grad_queries, remote_grads, own_grads = attend(
        ids, queries, out_grad, query_kv, passage_kv, queries_here, retrieved
    )
    chosen = (ids[:, None] == jnp.arange(owners * passages_here, dtype=jnp.int32)[None, :]).astype(
        jnp.bfloat16
    )
    dense = jnp.einsum("ep,exk->pxk", chosen, remote_grads, preferred_element_type=jnp.float32)
    dense = dense.astype(jnp.bfloat16).reshape(owners * rows_local, local_width)
    grad_kv = ring_sum(dense, chips, 2, jnp.bfloat16)
    full = jnp.zeros((rows_local, shares * local_width), jnp.bfloat16)
    full = lax.dynamic_update_slice_in_dim(full, grad_kv, share * local_width, axis=1)
    for k in range(1, shares):
        route = [(i, (i + k) % shares) for i in range(shares)]
        block = lax.ppermute(grad_kv, "tp", route)
        origin = lax.rem(share + shares - k, shares)
        full = lax.dynamic_update_slice_in_dim(full, block, origin * local_width, axis=1)
    partial = jnp.einsum("rc,rd->cd", full, passage_hidden, preferred_element_type=jnp.float32)
    weight_grad = ring_sum(partial.astype(jnp.bfloat16), chips, 3, jnp.float32)
    return grad_queries, own_grads, weight_grad


def solution(mesh):
    in_specs = (
        P("pas", "tp"),
        P("pas", "tp"),
        P("pas", "tp"),
        P("pas", "tp"),
        P("pas", "tp"),
        P("pas", None),
        P("pas", None),
    )
    out_specs = (P("pas", "tp"), P("pas", "tp"), P("pas", "tp"))
    return jax.shard_map(
        per_device, mesh=mesh, in_specs=in_specs, out_specs=out_specs, check_vma=False
    )
```

time: 869 us -> 454 us (0.52)
  waiting for transfers between devices: 646 us -> 69.5 us
  Pallas kernels: 0 us -> 314 us
  local copies, waits for them, and re-layouts: 76.8 us -> 23.2 us
  matrix products: 88.3 us -> 43.4 us
  other arithmetic: 31.7 us -> 0.01 us
  between operations: 13.8 us -> 0.78 us
    pallas_call x0 -> x5, Pallas kernels: none -> 314 us  [the longest x2 133 us: ring_gather(): pl.pallas_call(functools.partial(gather_kernel, chips, lanes), out_shape=...]
    all_gather x3 -> x0, waiting for transfers between devices: 264 us -> none  [the longest x1 119 us: per_device(): piece_rows = lax.all_gather(passage_kv, 'pas', axis=0, tiled=True)]
    reduce_scatter x2 -> x0, waiting for transfers between devices: 231 us -> none  [the longest x1 179 us: per_device(): lax.psum_scatter(jnp.einsum('rc,rd->cd', full_grad, passage_hidden, prefe...]
    all_to_all x2 -> x0, waiting for transfers between devices: 150 us -> none  [the longest x1 150 us: per_device(): lax.all_to_all(outgoing_grads, 'pas', split_axis=0, concat_axis=0, tiled=...]
    ppermute x0 -> x2, waiting for transfers between devices: none -> 69.5 us  [the longest x1 46.5 us: per_device(): lax.ppermute(project(lax.rem(share + k, shares)), 'tp', route)]
    dot_general x23 -> x4, matrix products: 66.4 us -> 43.4 us  [the longest x2 19.7 us: project(): lax.dot_general(passage_hidden, rows, (((1,), (1,)), ((), ())), preferred...]
    convert_element_type x7 -> x0, other arithmetic: 22.6 us -> none  [the longest x4 19.9 us: attend_block(): weights_low = weights.astype(jnp.bfloat16)]
    scatter x2 -> x0, local copies, waits for them, and re-layouts: 22.6 us -> none  [per_device(): outgoing_grads.at[flat_device, ranking]]
  transfers between devices with their start and end apart: 7 -> 2, of which waited for: 6 -> 2; matrix products, arithmetic and copies ran while one was open for 18% -> 0% of each run, Pallas kernels for 0% -> 0%
where the time goes in v1:
time: 454 us
  Pallas kernels  314 us (69%)
  waiting for transfers between devices  69.5 us (15%)
  matrix products  43.4 us (10%)
  local copies, waits for them, and re-layouts  23.2 us (5%)
    pallas_call x2, Pallas kernels, ring_gather(): pl.pallas_call(functools.partial(gather_kernel, chips, lanes), out_shape=...  133 us
    pallas_call x2, Pallas kernels, ring_sum(): pl.pallas_call(functools.partial(sum_kernel, chips, lanes), out_shape=jax...  131 us
    pallas_call x1, Pallas kernels, attend(): pl.pallas_call(functools.partial(attend_kernel, group, retrieved), grid_s...  50.3 us
    ppermute x1, waiting for transfers between devices, per_device(): lax.ppermute(project(lax.rem(share + k, shares)), 'tp', route)  46.5 us
    ppermute x1, waiting for transfers between devices, per_device(): block = lax.ppermute(grad_kv, 'tp', route)  23 us
    dot_general x2, matrix products, project(): lax.dot_general(passage_hidden, rows, (((1,), (1,)), ((), ())), preferred...  19.7 us
    convert_element_type x1, local copies, waits for them, and re-layouts, per_device(): dense = dense.astype(jnp.bfloat16).reshape(owners * rows_local, local_width)  18.5 us
    dot_general x1, matrix products, per_device(): jnp.einsum('ep,exk->pxk', chosen, remote_grads, preferred_element_type=jn...  12.5 us
  transfers between devices with their start and end apart: 2, of which 2 were waited for; matrix products, arithmetic and copies ran while one was open for 0% of the time, Pallas kernels for 0%

profile of v1, /device:TPU:0, one launch (start us, length us, event | category | flops | bytes accessed | tf_op | source)
XLA Modules:
  0.0 453.9 jit_solution(10176853703004920414)
XLA Ops:
  0.6 48.5 %shard_map.94 = bf16[8,2,2,2,16,4096]{5,4,3,2,1,0:T(8,128)(2,1)} custom-call(bf16[2,2,16,4096]{3,2,1,0:T(8,128)(2,1)} %bitcast.37), custom_call_target="tpu_custom_call" | custom-call | tf_op jit(solution)/shard_map/pallas_call | solution.py:94
  49.1 0.0 copy-start.3
  49.1 0.0 copy-start.4
  49.1 10.5 %fusion.8 = f32[1024,512]{0,1:T(8,128)} fusion(bf16[1024,4096]{1,0:T(8,128)(2,1)} %param.7, bf16[1024,4096]{1,0:T(8,128)(2,1)} %bitcast.34, s32[]{:T(128)S(6)} %select_n.9), kind=kOutput, calls=%fused_computation.9 | convolution fusion | flops 4294967296 | bytes 14680068 | tf_op jit(solution)/shard_map/dot_general | solution.py:313
  59.7 1.5 collective-permute-start
  61.2 0.0 copy-done.3
  61.2 0.0 copy-done.4
  61.2 0.1 reshape.28.ids_ref
  61.3 46.5 %collective-permute-done = f32[1024,512]{0,1:T(8,128)S(1)} collective-permute-done((f32[1024,512]{0,1:T(8,128)}, f32[1024,512]{0,1:T(8,128)S(1)}, u32[]{:S(2)}, u32[]{:S(2)}) %collective-permute-start) | collective-permute-done | bytes 2097184 | tf_op jit(solution)/shard_map/ppermute | solution.py:320
  107.8 9.2 %fusion.5 = bf16[1024,512]{0,1:T(8,128)(2,1)S(1)} fusion(f32[1024,512]{0,1:T(8,128)S(1)} %collective-permute-done, bf16[1024,4096]{1,0:T(8,128)(2,1)} %param.7, bf16[1024,4096]{1,0:T(8,128)(2,1)} %bitcast.35, s32[]{:T(128)S(6)} %select_n.8), kind=kOutput, calls=%fused_computation.8 | convolution fusion | flops 4296015872 | bytes 15728644 | tf_op jit(solution)/shard_map/dot_general | solution.py:313
  117.0 1.5 copy.10
  118.5 0.0 copy-start
  118.5 0.0 copy-start.2
  118.5 84.4 %shard_map.95 = bf16[8,2,2,2,256,512]{5,4,3,2,1,0:T(8,128)(2,1)} custom-call(bf16[2,2,256,512]{3,2,1,0:T(8,128)(2,1)} %bitcast.36), custom_call_target="tpu_custom_call" | custom-call | tf_op jit(solution)/shard_map/pallas_call | solution.py:94
  202.9 0.0 copy-done
  202.9 0.0 copy-done.2
  202.9 0.0 copy-start.1
  202.9 1.6 copy-done.1
  204.5 50.3 %shard_map.96 = (bf16[512,2048]{1,0:T(8,128)(2,1)}, bf16[32,128,512]{2,1,0:T(8,128)(2,1)}, bf16[512,512]{1,0:T(8,128)(2,1)}) custom-call(s32[32]{0:T(128)S(1)} %reshape.28.ids_ref, bf16[512,2048]{1,0:T(8,128)(2,1)S(1)} %copy-done, bf16[512,2048]{1,0:T(8,128)(2,1)S(1)} %copy-done.1, bf16[512,512]{1,0:T(8,128)(2,1)S(1)} %copy-done.2, ...), custom_call_target="tpu_custom_call" | custom-call | flops 14495514624 | bytes 16777216 | tf_op jit(solution)/shard_map/pallas_call | solution.py:272
  254.8 12.5 %convolution_convert_fusion = bf16[128,128,512]{2,0,1:T(8,128)(2,1)} fusion(bf16[32,128,512]{2,1,0:T(8,128)(2,1)} %get-tuple-element.8, s32[32]{0:T(128)S(1)} %reshape.28.ids_ref), kind=kOutput, calls=%fused_computation | convolution fusion | flops 545263616 | bytes 20971648 | tf_op jit(solution)/shard_map/ep,exk->pxk/dot_general | solution.py:333
  267.3 18.5 %copy.12 = bf16[128,128,512]{2,1,0:T(8,128)(2,1)} copy(bf16[128,128,512]{2,0,1:T(8,128)(2,1)} %convolution_convert_fusion) | data formatting | bytes 33554432 | tf_op jit(solution)/shard_map/convert_element_type | solution.py:334
  285.8 0.0 slice-start
  285.8 0.0 slice-start.1
  285.8 85.8 %shard_map.97 = bf16[2,2,256,512]{3,2,1,0:T(8,128)(2,1)S(1)} custom-call(bf16[8,2,2,2,256,512]{5,4,3,2,1,0:T(8,128)(2,1)} %bitcast.32), custom_call_target="tpu_custom_call" | custom-call | tf_op jit(solution)/shard_map/pallas_call | solution.py:185
  371.6 1.6 collective-permute-start.1
  373.2 0.3 broadcast_in_dim.4
  373.5 0.2 constant_dynamic-update-slice_fusion.1
  373.6 23.0 %collective-permute-done.1 = bf16[1024,512]{1,0:T(8,128)(2,1)S(1)} collective-permute-done((bf16[1024,512]{1,0:T(8,128)(2,1)S(1)}, bf16[1024,512]{1,0:T(8,128)(2,1)S(1)}, u32[]{:S(2)}, u32[]{:S(2)}) %collective-permute-start.1) | collective-permute-done | bytes 1048608 | tf_op jit(solution)/shard_map/ppermute | solution.py:340
  396.6 0.2 constant_dynamic-update-slice_fusion
  396.8 0.0 slice-done
  396.8 0.0 slice-done.1
  396.8 11.2 %convolution_convert_fusion.1 = bf16[1024,4096]{1,0:T(8,128)(2,1)} fusion(bf16[1024,1024]{1,0:T(8,128)(2,1)S(1)} %constant_dynamic-update-slice_fusion, bf16[1024,4096]{1,0:T(8,128)(2,1)S(1)} %bitcast.39), kind=kOutput, calls=%fused_computation.1 | convolution fusion | flops 8594128896 | bytes 18874368 | tf_op jit(solution)/shard_map/rc,rd->cd/dot_general | solution.py:343
  408.0 44.9 %shard_map.98 = f32[2,2,16,4096]{3,2,1,0:T(8,128)S(1)} custom-call(bf16[8,2,2,2,16,4096]{5,4,3,2,1,0:T(8,128)(2,1)} %bitcast.33), custom_call_target="tpu_custom_call" | custom-call | tf_op jit(solution)/shard_map/pallas_call | solution.py:185
  452.9 1.0 copy.18
  (2 shorter events, 0.0 us)
Async XLA Ops:
  49.1 12.0 %copy-start.3 = (s32[4,8]{1,0:T(4,128)S(1)}, s32[4,8]{1,0:T(4,128)}, u32[]{:S(2)}) copy-start(s32[4,8]{1,0:T(4,128)} %param.13) | copy-start | bytes 388
  49.1 12.0 %copy-start.4 = (s32[4,8]{1,0:T(4,128)S(1)}, s32[4,8]{1,0:T(4,128)}, u32[]{:S(2)}) copy-start(s32[4,8]{1,0:T(4,128)} %param.12) | copy-start | bytes 388
  59.7 48.1 %collective-permute-start = (f32[1024,512]{0,1:T(8,128)}, f32[1024,512]{0,1:T(8,128)S(1)}, u32[]{:S(2)}, u32[]{:S(2)}) collective-permute-start(f32[1024,512]{0,1:T(8,128)} %fusion.8), channel_id=1, source_target_pairs={{0,1},{1,0},{2,3},{3,2},{4,5},{5,4},{6,7},{7,6},{8,9},{9,8},{10,11... | collective-permute-start | bytes 6291464 | tf_op jit(solution)/shard_map/ppermute | solution.py:320
  118.5 84.4 %copy-start = (bf16[512,2048]{1,0:T(8,128)(2,1)S(1)}, bf16[512,2048]{1,0:T(8,128)(2,1)}, u32[]{:S(2)}) copy-start(bf16[512,2048]{1,0:T(8,128)(2,1)} %q_ref.1) | copy-start | bytes 6291460
  118.5 84.4 %copy-start.2 = (bf16[512,512]{1,0:T(8,128)(2,1)S(1)}, bf16[512,512]{1,0:T(8,128)(2,1)}, u32[]{:S(2)}) copy-start(bf16[512,512]{1,0:T(8,128)(2,1)} %own_ref.1) | copy-start | bytes 1572868
  202.9 1.6 copy-start.1
  285.8 111.0 %slice-start = ((s8[8388608]{0:T(1024)(128)(4,1)}), s8[4194304]{0:T(1024)(128)(4,1)S(1)}, s32[]{:S(2)}) async-start(s8[8388608]{0:T(1024)(128)(4,1)} %bitcast.38), calls=%async_computation | async-start | bytes 8388608
  285.8 111.0 %slice-start.1 = ((s8[8388608]{0:T(1024)(128)(4,1)}), s8[4194304]{0:T(1024)(128)(4,1)S(1)}, s32[]{:S(2)}) async-start(s8[8388608]{0:T(1024)(128)(4,1)} %bitcast.38), calls=%async_computation.1 | async-start | bytes 8388608
  371.6 25.0 %collective-permute-start.1 = (bf16[1024,512]{1,0:T(8,128)(2,1)S(1)}, bf16[1024,512]{1,0:T(8,128)(2,1)S(1)}, u32[]{:S(2)}, u32[]{:S(2)}) collective-permute-start(bf16[1024,512]{1,0:T(8,128)(2,1)S(1)} %bitcast.21), channel_id=1, source_target_pairs={{0,1},{1,0},{2,3},{3,2},{4,5},{5,4},{6,7},{7,6},{8,9},{9,8},{10,11... | collective-permute-start | bytes 3145736 | tf_op jit(solution)/shard_map/ppermute | solution.py:340

commit v2 on v1

--- a/solution.py
+++ b/solution.py
@@ -28,22 +28,20 @@
     return core, place, chip_at
 
 
-def greet(others):
+def greet(others, shares=()):
     barrier = pltpu.get_barrier_semaphore()
-    for other in others:
-        pl.semaphore_signal(
-            barrier, inc=1, device_id={"pas": other}, device_id_type=pl.DeviceIdType.MESH
-        )
-    pl.semaphore_wait(barrier, len(others))
-
-
-def send(src, dst, send_sem, recv_sem, other):
+    for place in [{"pas": other} for other in others] + [{"tp": other} for other in shares]:
+        pl.semaphore_signal(barrier, inc=1, device_id=place, device_id_type=pl.DeviceIdType.MESH)
+    pl.semaphore_wait(barrier, len(others) + len(shares))
+
+
+def send(src, dst, send_sem, recv_sem, other, axis="pas"):
     return pltpu.make_async_remote_copy(
         src_ref=src,
         dst_ref=dst,
         send_sem=send_sem,
         recv_sem=recv_sem,
-        device_id={"pas": other},
+        device_id={axis: other},
         device_id_type=pl.DeviceIdType.MESH,
     )
 
@@ -106,6 +104,165 @@
         compiler_params=pltpu.CompilerParams(collective_id=collective_id, has_side_effects=True),
     )(x.reshape(2, lanes, high, width))
     return out.reshape(chips * 2 * rows, width)
+
+
+def project_kernel(
+    chips, shares, lanes, hidden_ref, x_ref, out_ref, hidden, weight, joined, part, got,
+    own_sem, hidden_sem, ring_send, ring_recv, pair_send, pair_recv, share_send, share_recv,
+):
+    core, place, chip_at = ring_place(chips)
+    share = lax.axis_index("tp")
+    mine = chip_at(place)
+    partner = 2 * mine + 1 - core
+    nexts = (2 * chip_at(place + 1) + core, 2 * chip_at(place - 1) + core)
+    load = pltpu.make_async_copy(hidden_ref, hidden, hidden_sem)
+    load.start()
+    own = pltpu.make_async_copy(x_ref, weight.at[mine, core], own_sem)
+    own.start()
+    greet(
+        (nexts[0], nexts[1], partner),
+        [lax.rem(share + k, shares) for k in range(1, shares)],
+    )
+    rows = hidden.shape[0]
+    tile = min(256, rows)
+    half = part.shape[2]
+    each = half // 2
+    group = chips // shares
+    rings, pairs = {}, {}
+
+    def chip_of(step, way):
+        return chip_at(place - step if way == 0 else place + step)
+
+    def goal(step, way):
+        return lax.div(chip_of(step, way), group)
+
+    def share_copy(step, way):
+        target = goal(step, way)
+        slot = lax.rem(target - share + 2 * shares - 1, shares)
+        slot = lax.rem(slot, shares - 1)
+        return send(
+            part.at[way, step],
+            got.at[slot, way, step],
+            share_send.at[way, step],
+            share_recv.at[slot, way, step],
+            target,
+            "tp",
+        )
+
+    def multiply(step):
+        for way in range(2):
+            for lane in range(lanes):
+                pairs[step, way, lane].wait_recv()
+            piece = weight[chip_of(step, way), :, way]
+            joined[way * half : (way + 1) * half, :] = piece.reshape(half, piece.shape[-1])
+
+        def one(index, carry):
+            here = pl.ds(pl.multiple_of(index * tile, tile), tile)
+            product = lax.dot_general(
+                joined[...], hidden[here, :], (((1,), (1,)), ((), ())),
+                preferred_element_type=jnp.float32,
+            )
+            part[0, step, :, here] = product[:half]
+            part[1, step, :, here] = product[half:]
+            return carry
+
+        lax.fori_loop(0, rows // tile, one, 0)
+        for way in range(2):
+
+            @pl.when(goal(step, way) != share)
+            def _(way=way):
+                share_copy(step, way).start()
+
+    for step in range(chips):
+        for lane in range(lanes):
+            for way in range(2):
+                slot = weight.at[chip_of(step, way), core, way, lane]
+                if step == 0:
+                    src = x_ref.at[way, lane]
+                else:
+                    rings[step - 1, way, lane].wait_recv()
+                    src = slot
+                if step < chips - 1:
+                    copy = send(
+                        src, slot, ring_send.at[step, way, lane], ring_recv.at[step, way, lane], nexts[way]
+                    )
+                    copy.start()
+                    rings[step, way, lane] = copy
+                copy = send(
+                    src, slot, pair_send.at[step, way, lane], pair_recv.at[step, way, lane], partner
+                )
+                copy.start()
+                pairs[step, way, lane] = copy
+        if step == 0:
+            load.wait()
+            own.wait()
+        else:
+            multiply(step - 1)
+    multiply(chips - 1)
+    for step in range(chips):
+        for way in range(2):
+
+            @pl.when(goal(step, way) == share)
+            def _(step=step, way=way):
+                total = part[way, step]
+                for slot in range(shares - 1):
+                    send(
+                        part.at[way, step],
+                        got.at[slot, way, step],
+                        share_send.at[way, step],
+                        share_recv.at[slot, way, step],
+                        lax.rem(share + 1, shares),
+                        "tp",
+                    ).wait_recv()
+                    total = total + got[slot, way, step]
+                total = total.astype(out_ref.dtype)
+                where = lax.rem(chip_of(step, way), group)
+                out_ref[where, 0, way] = total[:each]
+                out_ref[where, 1, way] = total[each:]
+
+            @pl.when(goal(step, way) != share)
+            def _(step=step, way=way):
+                share_copy(step, way).wait_send()
+
+    for copy in rings.values():
+        copy.wait_send()
+    for copy in pairs.values():
+        copy.wait_send()
+
+
+def project(hidden, kv_weight, chips, shares, collective_id):
+    rows, width = hidden.shape
+    high = kv_weight.shape[0]
+    lanes = 2 if high % 64 == 0 else 1
+    high = high // (2 * lanes)
+    half = 2 * lanes * high
+    group = chips // shares
+    step_sems = pltpu.SemaphoreType.DMA((chips, 2, lanes))
+    out = pl.pallas_call(
+        functools.partial(project_kernel, chips, shares, lanes),
+        out_shape=jax.ShapeDtypeStruct((group, 2, 2, lanes * high, rows), jnp.bfloat16),
+        in_specs=[pl.BlockSpec(memory_space=pl.ANY)] * 2,
+        out_specs=pl.BlockSpec(memory_space=pltpu.VMEM),
+        scratch_shapes=[
+            pltpu.VMEM((rows, width), hidden.dtype),
+            pltpu.VMEM((chips, 2, 2, lanes, high, width), kv_weight.dtype),
+            pltpu.VMEM((2 * half, width), kv_weight.dtype),
+            pltpu.VMEM((2, chips, half, rows), jnp.float32),
+            pltpu.VMEM((shares - 1, 2, chips, half, rows), jnp.float32),
+            pltpu.SemaphoreType.DMA,
+            pltpu.SemaphoreType.DMA,
+            step_sems,
+            step_sems,
+            step_sems,
+            step_sems,
+            pltpu.SemaphoreType.DMA((2, chips)),
+            pltpu.SemaphoreType.DMA((shares - 1, 2, chips)),
+        ],
+        compiler_params=pltpu.CompilerParams(
+            collective_id=collective_id, has_side_effects=True, vmem_limit_bytes=56 * MIB
+        ),
+    )(hidden, kv_weight.reshape(2, lanes, high, width))
+    return out.reshape(group * 2 * 2 * lanes * high, rows).T
 
 
 def sum_kernel(
@@ -206,10 +363,20 @@
 
 def attend_kernel(group, retrieved, ids_ref, q_ref, g_ref, own_ref, *refs):
     passages = refs[:retrieved]
-    dq_ref, remote_ref, down_ref, keys, values, dkeys, dvalues = refs[retrieved:]
+    dq_ref, dense_ref, down_ref, keys, values, dkeys, dvalues = refs[retrieved:]
     scaling = HD ** (-0.5)
     remote = retrieved * PLEN
     tokens = q_ref.shape[0]
+    query = pl.program_id(1)
+
+    @pl.when(query == 0)
+    def _():
+        def clear(p, carry):
+            dense_ref[p] = jnp.zeros(dense_ref.shape[1:], dense_ref.dtype)
+            return carry
+
+        lax.fori_loop(0, dense_ref.shape[0], clear, 0)
+
     for i in range(retrieved):
         keys[i * PLEN : (i + 1) * PLEN, :] = passages[i][0, :, :HD]
         values[i * PLEN : (i + 1) * PLEN, :] = passages[i][0, :, HD:]
@@ -249,8 +416,11 @@
             dkeys[...] += dk
             dvalues[...] += dv
     for i in range(retrieved):
-        remote_ref[i, :, :HD] = (dkeys[i * PLEN : (i + 1) * PLEN, :] * scaling).astype(remote_ref.dtype)
-        remote_ref[i, :, HD:] = dvalues[i * PLEN : (i + 1) * PLEN, :].astype(remote_ref.dtype)
+        p = ids_ref[query * retrieved + i]
+        rows = slice(i * PLEN, (i + 1) * PLEN)
+        pair = jnp.concatenate([dkeys[rows, :] * scaling, dvalues[rows, :]], axis=1)
+        pair = pair.astype(jnp.bfloat16).astype(jnp.float32)
+        dense_ref[p] = (dense_ref[p].astype(jnp.float32) + pair).astype(dense_ref.dtype)
     down_ref[:, :HD] = (dkeys[remote:, :] * scaling).astype(down_ref.dtype)
     down_ref[:, HD:] = dvalues[remote:, :].astype(down_ref.dtype)
 
@@ -264,20 +434,20 @@
     keys = retrieved * PLEN + tokens
 
     def passage_spec(i):
-        return pl.BlockSpec((1, PLEN, 2 * HD), lambda n, h, ids: (ids[n * retrieved + i], 0, h))
-
-    wide_spec = pl.BlockSpec((tokens, wide), lambda n, h, ids: (n, h))
-    own_spec = pl.BlockSpec((tokens, 2 * HD), lambda n, h, ids: (n, h))
+        return pl.BlockSpec((1, PLEN, 2 * HD), lambda h, n, ids: (ids[n * retrieved + i], 0, h))
+
+    wide_spec = pl.BlockSpec((tokens, wide), lambda h, n, ids: (n, h))
+    own_spec = pl.BlockSpec((tokens, 2 * HD), lambda h, n, ids: (n, h))
     flops = 12 * queries_here * heads * group * tokens * keys * HD
     return pl.pallas_call(
         functools.partial(attend_kernel, group, retrieved),
         grid_spec=pltpu.PrefetchScalarGridSpec(
             num_scalar_prefetch=1,
-            grid=(queries_here, heads),
+            grid=(heads, queries_here),
             in_specs=[wide_spec, wide_spec, own_spec] + [passage_spec(i) for i in range(retrieved)],
             out_specs=[
                 wide_spec,
-                pl.BlockSpec((retrieved, PLEN, 2 * HD), lambda n, h, ids: (n, 0, h)),
+                pl.BlockSpec((passage_kv.shape[0], PLEN, 2 * HD), lambda h, n, ids: (0, 0, h)),
                 own_spec,
             ],
             scratch_shapes=[
@@ -289,10 +459,10 @@
         ),
         out_shape=[
             jax.ShapeDtypeStruct(queries.shape, jnp.bfloat16),
-            jax.ShapeDtypeStruct((queries_here * retrieved, PLEN, width), jnp.bfloat16),
+            jax.ShapeDtypeStruct(passage_kv.shape, jnp.bfloat16),
             jax.ShapeDtypeStruct(query_kv.shape, jnp.bfloat16),
         ],
-        compiler_params=pltpu.CompilerParams(vmem_limit_bytes=48 * MIB),
+        compiler_params=pltpu.CompilerParams(vmem_limit_bytes=56 * MIB),
         cost_estimate=pl.CostEstimate(flops=flops, bytes_accessed=16 * MIB, transcendentals=0),
     )(ids, queries, out_grad, query_kv, *([passage_kv] * retrieved))
 
@@ -306,32 +476,14 @@
     local_width = query_kv.shape[1]
     passages_here = rows_local // PLEN
     queries_here, retrieved = source_device.shape
-    weight = ring_gather(kv_weight, chips, 0)
-
-    def project(target):
-        rows = lax.dynamic_slice_in_dim(weight, target * local_width, local_width, axis=0)
-        return lax.dot_general(
-            passage_hidden, rows, (((1,), (1,)), ((), ())), preferred_element_type=jnp.float32
-        )
-
-    arrived = []
-    for k in range(1, shares):
-        route = [(i, (i + k) % shares) for i in range(shares)]
-        arrived.append(lax.ppermute(project(lax.rem(share + k, shares)), "tp", route))
-    projected = project(share)
-    for block in arrived:
-        projected = projected + block
-    passage_kv = ring_gather(projected.astype(jnp.bfloat16), chips, 1)
+    projected = project(passage_hidden, kv_weight, chips, shares, 0)
+    passage_kv = ring_gather(projected, chips, 1)
     passage_kv = passage_kv.reshape(owners * passages_here, PLEN, local_width)
     ids = (source_device * passages_here + source_slot).reshape(-1)
-    grad_queries, remote_grads, own_grads = attend(
+    grad_queries, dense, own_grads = attend(
         ids, queries, out_grad, query_kv, passage_kv, queries_here, retrieved
     )
-    chosen = (ids[:, None] == jnp.arange(owners * passages_here, dtype=jnp.int32)[None, :]).astype(
-        jnp.bfloat16
-    )
-    dense = jnp.einsum("ep,exk->pxk", chosen, remote_grads, preferred_element_type=jnp.float32)
-    dense = dense.astype(jnp.bfloat16).reshape(owners * rows_local, local_width)
+    dense = dense.reshape(owners * rows_local, local_width)
     grad_kv = ring_sum(dense, chips, 2, jnp.bfloat16)
     full = jnp.zeros((rows_local, shares * local_width), jnp.bfloat16)
     full = lax.dynamic_update_slice_in_dim(full, grad_kv, share * local_width, axis=1)

time: 454 us -> 390 us (0.86)
  waiting for transfers between devices: 69.5 us -> 24.2 us
  Pallas kernels: 314 us -> 345 us
  matrix products: 43.4 us -> 14.8 us
  local copies, waits for them, and re-layouts: 23.2 us -> 4.5 us
    pallas_call x0 -> x1, Pallas kernels: none -> 72.6 us  [project(): pl.pallas_call(functools.partial(project_kernel, chips, shares, lanes), o...]
    pallas_call x2 -> x1, Pallas kernels: 133 us -> 84.8 us  [ring_gather(): pl.pallas_call(functools.partial(gather_kernel, chips, lanes), out_shape=...]
    ppermute x1 -> x0, waiting for transfers between devices: 46.5 us -> none  [per_device(): lax.ppermute(project(lax.rem(share + k, shares)), 'tp', route)]
    dot_general x3 -> x0, matrix products: 32.2 us -> none  [the longest x2 19.7 us: project(): lax.dot_general(passage_hidden, rows, (((1,), (1,)), ((), ())), preferred...]
    convert_element_type x2 -> x0, local copies, waits for them, and re-layouts: 20 us -> none  [the longest x1 18.5 us: per_device(): dense = dense.astype(jnp.bfloat16).reshape(owners * rows_local, local_width)]
  transfers between devices with their start and end apart: 2 -> 1, of which waited for: 2 -> 1; matrix products, arithmetic and copies ran while one was open for 0% -> 0% of each run, Pallas kernels for 0% -> 0%
where the time goes in v2:
time: 390 us
  Pallas kernels  345 us (88%)
  waiting for transfers between devices  24.2 us (6%)
  matrix products  14.8 us (4%)
  local copies, waits for them, and re-layouts  4.5 us (1%)
    pallas_call x2, Pallas kernels, ring_sum(): pl.pallas_call(functools.partial(sum_kernel, chips, lanes), out_shape=jax...  133 us
    pallas_call x1, Pallas kernels, ring_gather(): pl.pallas_call(functools.partial(gather_kernel, chips, lanes), out_shape=...  84.8 us
    pallas_call x1, Pallas kernels, project(): pl.pallas_call(functools.partial(project_kernel, chips, shares, lanes), o...  72.6 us
    pallas_call x1, Pallas kernels, attend(): pl.pallas_call(functools.partial(attend_kernel, group, retrieved), grid_s...  54.4 us
    ppermute x1, waiting for transfers between devices, per_device(): block = lax.ppermute(grad_kv, 'tp', route)  24.2 us
    dot_general x1, matrix products, per_device(): jnp.einsum('rc,rd->cd', full, passage_hidden, preferred_element_type=jnp....  14.8 us
  transfers between devices with their start and end apart: 1, of which 1 were waited for; matrix products, arithmetic and copies ran while one was open for 0% of the time, Pallas kernels for 0%

profile of v2, /device:TPU:0, one launch (start us, length us, event | category | flops | bytes accessed | tf_op | source)
XLA Modules:
  0.0 390.2 jit_solution(4776741898211736882)
XLA Ops:
  0.6 0.7 multiply_add_fusion
  1.3 0.7 reshape.27.ids_ref
  2.0 72.6 %shard_map.94 = bf16[4,2,2,32,1024]{4,3,2,1,0:T(8,128)(2,1)} custom-call(bf16[1024,4096]{1,0:T(8,128)(2,1)} %hidden_ref.1, bf16[2,2,16,4096]{3,2,1,0:T(8,128)(2,1)} %bitcast.27), custom_call_target="tpu_custom_call" | custom-call | tf_op jit(solution)/shard_map/pallas_call | solution.py:241
  74.6 2.3 copy.10
  76.9 84.8 %shard_map.95 = bf16[8,2,2,2,256,512]{5,4,3,2,1,0:T(8,128)(2,1)} custom-call(bf16[2,2,256,512]{3,2,1,0:T(8,128)(2,1)} %bitcast.25), custom_call_target="tpu_custom_call" | custom-call | tf_op jit(solution)/shard_map/pallas_call | solution.py:92
  161.8 54.4 %shard_map.96 = (bf16[512,2048]{1,0:T(8,128)(2,1)}, bf16[128,128,512]{2,1,0:T(8,128)(2,1)}, bf16[512,512]{1,0:T(8,128)(2,1)}) custom-call(s32[32]{0:T(128)} %reshape.27.ids_ref, bf16[512,2048]{1,0:T(8,128)(2,1)} %q_ref.1, bf16[512,2048]{1,0:T(8,128)(2,1)} %g_ref.1, bf16[512,512]{1,0:T(8,128)(2,1)} %own_ref.1, bf16[128,128,512]{2,1,0:T(8,128)(2,1)} %bitcast.15, ...), custom_call_target="tpu_custom_call" | custom-call | flops 14495514624 | bytes 16777216 | tf_op jit(solution)/shard_map/pallas_call | solution.py:442
  216.1 88.0 %shard_map.97 = bf16[2,2,256,512]{3,2,1,0:T(8,128)(2,1)S(1)} custom-call(bf16[8,2,2,2,256,512]{5,4,3,2,1,0:T(8,128)(2,1)} %bitcast.23), custom_call_target="tpu_custom_call" | custom-call | tf_op jit(solution)/shard_map/pallas_call | solution.py:342
  304.2 0.3 collective-permute-start
  304.5 0.3 broadcast_in_dim.3
  304.8 0.2 constant_dynamic-update-slice_fusion.1
  304.9 24.2 %collective-permute-done = bf16[1024,512]{1,0:T(8,128)(2,1)S(1)} collective-permute-done((bf16[1024,512]{1,0:T(8,128)(2,1)S(1)}, bf16[1024,512]{1,0:T(8,128)(2,1)S(1)}, u32[]{:S(2)}, u32[]{:S(2)}) %collective-permute-start) | collective-permute-done | bytes 1048608 | tf_op jit(solution)/shard_map/ppermute | solution.py:492
  329.2 0.2 constant_dynamic-update-slice_fusion
  329.3 14.8 %convolution_convert_fusion = bf16[1024,4096]{1,0:T(8,128)(2,1)} fusion(bf16[1024,1024]{1,0:T(8,128)(2,1)S(1)} %constant_dynamic-update-slice_fusion, bf16[1024,4096]{1,0:T(8,128)(2,1)} %hidden_ref.1), kind=kOutput, calls=%fused_computation | convolution fusion | flops 8594128896 | bytes 18874368 | tf_op jit(solution)/shard_map/rc,rd->cd/dot_general | solution.py:495
  344.1 45.1 %shard_map.98 = f32[2,2,16,4096]{3,2,1,0:T(8,128)S(1)} custom-call(bf16[8,2,2,2,16,4096]{5,4,3,2,1,0:T(8,128)(2,1)} %bitcast.24), custom_call_target="tpu_custom_call" | custom-call | tf_op jit(solution)/shard_map/pallas_call | solution.py:342
  389.2 1.0 copy.14
Async XLA Ops:
  304.2 25.0 %collective-permute-start = (bf16[1024,512]{1,0:T(8,128)(2,1)S(1)}, bf16[1024,512]{1,0:T(8,128)(2,1)S(1)}, u32[]{:S(2)}, u32[]{:S(2)}) collective-permute-start(bf16[1024,512]{1,0:T(8,128)(2,1)S(1)} %bitcast.12), channel_id=1, source_target_pairs={{0,1},{1,0},{2,3},{3,2},{4,5},{5,4},{6,7},{7,6},{8,9},{9,8},{10,11... | collective-permute-start | bytes 3145736 | tf_op jit(solution)/shard_map/ppermute | solution.py:492

commit v3 on v2

--- a/solution.py
+++ b/solution.py
@@ -265,100 +265,236 @@
     return out.reshape(group * 2 * 2 * lanes * high, rows).T
 
 
-def sum_kernel(
-    chips, lanes, x_ref, out_ref, mine, pair, got,
-    own_sem, pair_send, pair_recv, ring_send, ring_recv,
+def return_kernel(
+    chips, shares, lanes, thin, x_ref, hidden_ref, out_ref,
+    mine, pair, got, full, hidden, joined, ours, theirs, pair_low, got_low,
+    hidden_sem, own_sem, pair_send, pair_recv, ring_send, ring_recv, share_send, share_recv,
+    low_pair_send, low_pair_recv, low_ring_send, low_ring_recv,
 ):
     core, place, chip_at = ring_place(chips)
+    share = lax.axis_index("tp")
     partner = 2 * chip_at(place) + 1 - core
     nexts = (2 * chip_at(place + 1) + core, 2 * chip_at(place - 1) + core)
-    high = x_ref.shape[4]
-    part = 16
-    owns, pairs, rings = {}, {}, {}
-    greet((nexts[0], nexts[1], partner))
-    for step in range(chips):
-        for way in range(2):
-            ahead = place - 1 - step if way == 0 else place + 1 + step
-            where = chip_at(ahead)
-            copy = send(
-                x_ref.at[where, 1 - core, way],
-                pair.at[way, step],
-                pair_send.at[way, step],
-                pair_recv.at[way, step],
-                partner,
-            )
-            copy.start()
-            pairs[way, step] = copy
-            copy = pltpu.make_async_copy(
-                x_ref.at[where, core, way], mine.at[way, step], own_sem.at[way, step]
-            )
-            copy.start()
-            owns[way, step] = copy
-    for step in range(chips):
+    heads, _, _, _, high, wide = mine.shape
+    rows, width = hidden.shape
+    local = heads * wide
+    load = pltpu.make_async_copy(hidden_ref, hidden, hidden_sem)
+    owns, pairs, rings, sent = {}, {}, {}, []
+    greet(
+        (nexts[0], nexts[1], partner),
+        [lax.rem(share + k, shares) for k in range(1, shares)],
+    )
+
+    def chip_of(step, way):
+        return chip_at(place - 1 - step if way == 0 else place + 1 + step)
+
+    for head in range(heads):
+        columns = pl.ds(head * wide, wide)
+        for step in range(chips):
+            for way in range(2):
+                where = chip_of(step, way)
+                copy = send(
+                    x_ref.at[where, 1 - core, way, :, :, columns],
+                    pair.at[head, way, step],
+                    pair_send.at[head, way, step],
+                    pair_recv.at[head, way, step],
+                    partner,
+                )
+                copy.start()
+                pairs[head, way, step] = copy
+                sent.append(copy)
+                copy = pltpu.make_async_copy(
+                    x_ref.at[where, core, way, :, :, columns],
+                    mine.at[head, way, step],
+                    own_sem.at[head, way, step],
+                )
+                copy.start()
+                owns[head, way, step] = copy
+    load.start()
+
+    def share_copy(head, origin, k):
+        slot = full.at[pl.ds(pl.multiple_of(origin * local + head * wide, wide), wide)]
+        return send(
+            slot, slot, share_send.at[head, k - 1], share_recv.at[head, k - 1],
+            lax.rem(share + k, shares), "tp",
+        )
+
+    def work(head, step):
         last = step == chips - 1
         for lane in range(lanes):
             for way in range(2):
                 if lane == 0:
-                    owns[way, step].wait()
-                    pairs[way, step].wait_recv()
+                    owns[head, way, step].wait()
+                    pairs[head, way, step].wait_recv()
                 if step > 0:
-                    rings[step - 1, way, lane].wait_recv()
+                    rings[head, step - 1, way, lane].wait_recv()
+                if last:
+                    total = mine[head, way, step, lane].astype(jnp.float32)
+                    total += pair[head, way, step, lane].astype(jnp.float32)
+                    total += got[head, way, step - 1, lane].astype(jnp.float32)
+                    start = pl.multiple_of(share * local + head * wide, wide)
+                    there = (way * lanes + lane) * high
+                    full[pl.ds(start, wide), there : there + high] = total.T.astype(full.dtype)
+                    continue
 
                 def add(index, carry, way=way, lane=lane):
-                    here = pl.ds(pl.multiple_of(index * part, part), part)
-                    total = mine[way, step, lane, here, :].astype(jnp.float32)
-                    total += pair[way, step, lane, here, :].astype(jnp.float32)
+                    here = pl.ds(pl.multiple_of(index * 32, 32), 32)
+                    total = mine[head, way, step, lane, here, :].astype(jnp.float32)
+                    total += pair[head, way, step, lane, here, :].astype(jnp.float32)
                     if step > 0:
-                        total += got[way, step - 1, lane, here, :].astype(jnp.float32)
+                        total += got[head, way, step - 1, lane, here, :].astype(jnp.float32)
+                    mine[head, way, step, lane, here, :] = total.astype(mine.dtype)
+                    return carry
+
+                lax.fori_loop(0, high // 32, add, 0)
+                copy = send(
+                    mine.at[head, way, step, lane],
+                    got.at[head, way, step, lane],
+                    ring_send.at[head, step, way, lane],
+                    ring_recv.at[head, step, way, lane],
+                    nexts[way],
+                )
+                copy.start()
+                rings[head, step, way, lane] = copy
+                sent.append(copy)
+        if last:
+            for k in range(1, shares):
+                copy = share_copy(head, share, k)
+                copy.start()
+                sent.append(copy)
+
+    for head in range(heads):
+        for step in range(chips):
+            if step == chips - 1 and head + 1 < heads:
+                work(head + 1, 0)
+            if step == 0 and head > 0:
+                continue
+            work(head, step)
+    load.wait()
+    for head in range(heads):
+        for k in range(1, shares):
+            share_copy(head, lax.rem(share + shares - k, shares), k).wait_recv()
+
+    each = joined.shape[0] // 4
+    short = each // thin
+    tile = min(512, width)
+    low_pairs, low_rings = {}, {}
+
+    def multiply(step):
+        for way in range(2):
+            for other in range(2):
+                side = core if other == 0 else 1 - core
+                start = ((2 * chip_of(step, way) + side) * 2 + way) * each
+                there = (2 * way + other) * each
+                joined[there : there + each, :] = full[pl.ds(pl.multiple_of(start, each), each), :]
+
+        def one(index, carry):
+            here = pl.ds(pl.multiple_of(index * tile, tile), tile)
+            product = jnp.dot(
+                joined[...], hidden[:, here], preferred_element_type=jnp.float32
+            ).astype(ours.dtype)
+            for way in range(2):
+                there = 2 * way * each
+                ours[way, step, :, here] = product[there : there + each]
+                theirs[way, step, :, here] = product[there + each : there + 2 * each]
+            return carry
+
+        lax.fori_loop(0, width // tile, one, 0)
+        for way in range(2):
+            copy = send(
+                theirs.at[way, step],
+                pair_low.at[way, step],
+                low_pair_send.at[way, step],
+                low_pair_recv.at[way, step],
+                partner,
+            )
+            copy.start()
+            low_pairs[way, step] = copy
+            sent.append(copy)
+
+    def pass_on(step):
+        last = step == chips - 1
+        for lane in range(thin):
+            for way in range(2):
+                if lane == 0:
+                    low_pairs[way, step].wait_recv()
+                if step > 0:
+                    low_rings[step - 1, way, lane].wait_recv()
+                here = slice(lane * short, (lane + 1) * short)
+
+                def add(index, carry, way=way, here=here):
+                    there = pl.ds(pl.multiple_of(index * tile, tile), tile)
+                    total = ours[way, step, here, there].astype(jnp.float32)
+                    total += pair_low[way, step, here, there].astype(jnp.float32)
+                    if step > 0:
+                        total += got_low[way, step - 1, here, there].astype(jnp.float32)
                     if last:
-                        out_ref[way, lane, here, :] = total.astype(out_ref.dtype)
+                        out_ref[way, here, there] = total
                     else:
-                        mine[way, step, lane, here, :] = total.astype(mine.dtype)
+                        ours[way, step, here, there] = total.astype(ours.dtype)
                     return carry
 
-                lax.fori_loop(0, high // part, add, 0)
+                lax.fori_loop(0, width // tile, add, 0)
                 if not last:
                     copy = send(
-                        mine.at[way, step, lane],
-                        got.at[way, step, lane],
-                        ring_send.at[step, way, lane],
-                        ring_recv.at[step, way, lane],
+                        ours.at[way, step, here],
+                        got_low.at[way, step, here],
+                        low_ring_send.at[step, way, lane],
+                        low_ring_recv.at[step, way, lane],
                         nexts[way],
                     )
                     copy.start()
-                    rings[step, way, lane] = copy
-    for copy in pairs.values():
+                    low_rings[step, way, lane] = copy
+                    sent.append(copy)
+
+    multiply(0)
+    for step in range(chips):
+        if step + 1 < chips:
+            multiply(step + 1)
+        pass_on(step)
+    for copy in sent:
         copy.wait_send()
-    for copy in rings.values():
-        copy.wait_send()
-
-
-def ring_sum(x, chips, collective_id, out_dtype):
-    rows, width = x.shape
-    rows = rows // (2 * chips)
-    lanes = 2 if rows % 64 == 0 else 1
+
+
+def return_grads(dense, hidden, chips, shares, out_rows, collective_id):
+    rows, width = hidden.shape
+    local = dense.shape[1]
+    wide = 2 * HD
+    heads = local // wide
+    lanes = 2
     high = rows // (2 * lanes)
-    block = (lanes, high, width)
+    each = out_rows // 2
+    thin = 2 if each % 32 == 0 else 1
+    slots = pltpu.VMEM((heads, 2, chips, lanes, high, wide), dense.dtype)
+    low_slots = pltpu.VMEM((2, chips, each, width), dense.dtype)
+    head_sems = pltpu.SemaphoreType.DMA((heads, 2, chips))
+    lane_sems = pltpu.SemaphoreType.DMA((heads, chips, 2, lanes))
+    share_sems = pltpu.SemaphoreType.DMA((heads, shares - 1))
+    low_sems = pltpu.SemaphoreType.DMA((2, chips))
+    thin_sems = pltpu.SemaphoreType.DMA((chips, 2, thin))
     out = pl.pallas_call(
-        functools.partial(sum_kernel, chips, lanes),
-        out_shape=jax.ShapeDtypeStruct((2,) + block, out_dtype),
-        in_specs=[pl.BlockSpec(memory_space=pl.ANY)],
+        functools.partial(return_kernel, chips, shares, lanes, thin),
+        out_shape=jax.ShapeDtypeStruct((2, each, width), jnp.float32),
+        in_specs=[pl.BlockSpec(memory_space=pl.ANY)] * 2,
         out_specs=pl.BlockSpec(memory_space=pltpu.VMEM),
         scratch_shapes=[
-            pltpu.VMEM((2, chips) + block, x.dtype),
-            pltpu.VMEM((2, chips) + block, x.dtype),
-            pltpu.VMEM((2, chips) + block, x.dtype),
-            pltpu.SemaphoreType.DMA((2, chips)),
-            pltpu.SemaphoreType.DMA((2, chips)),
-            pltpu.SemaphoreType.DMA((2, chips)),
-            pltpu.SemaphoreType.DMA((chips, 2, lanes)),
-            pltpu.SemaphoreType.DMA((chips, 2, lanes)),
+            slots, slots, slots,
+            pltpu.VMEM((shares * local, rows), dense.dtype),
+            pltpu.VMEM((rows, width), hidden.dtype),
+            pltpu.VMEM((4 * each, rows), dense.dtype),
+            low_slots, low_slots, low_slots, low_slots,
+            pltpu.SemaphoreType.DMA,
+            head_sems, head_sems, head_sems,
+            lane_sems, lane_sems,
+            share_sems, share_sems,
+            low_sems, low_sems,
+            thin_sems, thin_sems,
         ],
         compiler_params=pltpu.CompilerParams(
-            collective_id=collective_id, has_side_effects=True, vmem_limit_bytes=48 * MIB
+            collective_id=collective_id, has_side_effects=True, vmem_limit_bytes=60 * MIB
         ),
-    )(x.reshape((chips, 2, 2) + block))
-    return out.reshape(rows, width)
+    )(dense.reshape(chips, 2, 2, lanes, high, local), hidden)
+    return out.reshape(out_rows, width)
 
 
 def attend_kernel(group, retrieved, ids_ref, q_ref, g_ref, own_ref, *refs):
@@ -484,16 +620,7 @@
         ids, queries, out_grad, query_kv, passage_kv, queries_here, retrieved
     )
     dense = dense.reshape(owners * rows_local, local_width)
-    grad_kv = ring_sum(dense, chips, 2, jnp.bfloat16)
-    full = jnp.zeros((rows_local, shares * local_width), jnp.bfloat16)
-    full = lax.dynamic_update_slice_in_dim(full, grad_kv, share * local_width, axis=1)
-    for k in range(1, shares):
-        route = [(i, (i + k) % shares) for i in range(shares)]
-        block = lax.ppermute(grad_kv, "tp", route)
-        origin = lax.rem(share + shares - k, shares)
-        full = lax.dynamic_update_slice_in_dim(full, block, origin * local_width, axis=1)
-    partial = jnp.einsum("rc,rd->cd", full, passage_hidden, preferred_element_type=jnp.float32)
-    weight_grad = ring_sum(partial.astype(jnp.bfloat16), chips, 3, jnp.float32)
+    weight_grad = return_grads(dense, passage_hidden, chips, shares, kv_weight.shape[0], 2)
     return grad_queries, own_grads, weight_grad
 
 

time: 390 us -> 368 us (0.944)
  waiting for transfers between devices: 24.2 us -> 0 us
  Pallas kernels: 345 us -> 361 us
  matrix products: 14.8 us -> 0 us
    ppermute x1 -> x0, waiting for transfers between devices: 24.2 us -> none  [per_device(): block = lax.ppermute(grad_kv, 'tp', route)]
    pallas_call x2 -> x1, Pallas kernels: 133 us -> 149 us  [return_grads(): pl.pallas_call(functools.partial(return_kernel, chips, shares, lanes, thi...]
    dot_general x1 -> x0, matrix products: 14.8 us -> none  [per_device(): jnp.einsum('rc,rd->cd', full, passage_hidden, preferred_element_type=jnp....]
  transfers between devices with their start and end apart: 1 -> 0, of which waited for: 1 -> 0; matrix products, arithmetic and copies ran while one was open for 0% -> 0% of each run, Pallas kernels for 0% -> 0%
where the time goes in v3:
time: 368 us; the launch traced here: 367 us
  Pallas kernels  361 us (98%)
  local copies, waits for them, and re-layouts  5.36 us (1%)
    pallas_call x1, Pallas kernels, return_grads(): pl.pallas_call(functools.partial(return_kernel, chips, shares, lanes, thi...  149 us
    pallas_call x1, Pallas kernels, ring_gather(): pl.pallas_call(functools.partial(gather_kernel, chips, lanes), out_shape=...  84.8 us
    pallas_call x1, Pallas kernels, project(): pl.pallas_call(functools.partial(project_kernel, chips, shares, lanes), o...  72.5 us
    pallas_call x1, Pallas kernels, attend(): pl.pallas_call(functools.partial(attend_kernel, group, retrieved), grid_s...  54.4 us

profile of v3, /device:TPU:0, one launch (start us, length us, event | category | flops | bytes accessed | tf_op | source)
XLA Modules:
  0.0 367.4 jit_solution(8977358635756097541)
XLA Ops:
  0.6 0.7 multiply_add_fusion
  1.3 0.6 reshape.21.ids_ref
  2.0 72.5 %shard_map.94 = bf16[4,2,2,32,1024]{4,3,2,1,0:T(8,128)(2,1)} custom-call(bf16[1024,4096]{1,0:T(8,128)(2,1)} %hidden_ref.3, bf16[2,2,16,4096]{3,2,1,0:T(8,128)(2,1)} %bitcast.20), custom_call_target="tpu_custom_call" | custom-call | tf_op jit(solution)/shard_map/pallas_call | solution.py:241
  74.4 2.5 copy.10
  76.9 84.8 %shard_map.95 = bf16[8,2,2,2,256,512]{5,4,3,2,1,0:T(8,128)(2,1)} custom-call(bf16[2,2,256,512]{3,2,1,0:T(8,128)(2,1)} %bitcast.17), custom_call_target="tpu_custom_call" | custom-call | tf_op jit(solution)/shard_map/pallas_call | solution.py:92
  161.7 54.4 %shard_map.96 = (bf16[512,2048]{1,0:T(8,128)(2,1)}, bf16[128,128,512]{2,1,0:T(8,128)(2,1)}, bf16[512,512]{1,0:T(8,128)(2,1)}) custom-call(s32[32]{0:T(128)} %reshape.21.ids_ref, bf16[512,2048]{1,0:T(8,128)(2,1)} %q_ref.1, bf16[512,2048]{1,0:T(8,128)(2,1)} %g_ref.1, bf16[512,512]{1,0:T(8,128)(2,1)} %own_ref.1, bf16[128,128,512]{2,1,0:T(8,128)(2,1)} %bitcast.8, ...), custom_call_target="tpu_custom_call" | custom-call | flops 14495514624 | bytes 16777216 | tf_op jit(solution)/shard_map/pallas_call | solution.py:578
  216.1 149.0 %shard_map.97 = f32[2,32,4096]{2,1,0:T(8,128)} custom-call(bf16[8,2,2,2,256,512]{5,4,3,2,1,0:T(8,128)(2,1)} %bitcast.16, bf16[1024,4096]{1,0:T(8,128)(2,1)} %hidden_ref.3), custom_call_target="tpu_custom_call" | custom-call | tf_op jit(solution)/shard_map/pallas_call | solution.py:475
  365.1 2.3 copy.12

commit v4 on v3

--- a/solution.py
+++ b/solution.py
@@ -497,27 +497,18 @@
     return out.reshape(out_rows, width)
 
 
-def attend_kernel(group, retrieved, ids_ref, q_ref, g_ref, own_ref, *refs):
-    passages = refs[:retrieved]
-    dq_ref, dense_ref, down_ref, keys, values, dkeys, dvalues = refs[retrieved:]
+def attend_rows(
+    group, retrieved, rows, passage, q_ref, g_ref, own_ref, dq_ref, keys, values, dkeys, dvalues, between
+):
     scaling = HD ** (-0.5)
     remote = retrieved * PLEN
-    tokens = q_ref.shape[0]
-    query = pl.program_id(1)
-
-    @pl.when(query == 0)
-    def _():
-        def clear(p, carry):
-            dense_ref[p] = jnp.zeros(dense_ref.shape[1:], dense_ref.dtype)
-            return carry
-
-        lax.fori_loop(0, dense_ref.shape[0], clear, 0)
-
+    tokens = keys.shape[0] - remote
     for i in range(retrieved):
-        keys[i * PLEN : (i + 1) * PLEN, :] = passages[i][0, :, :HD]
-        values[i * PLEN : (i + 1) * PLEN, :] = passages[i][0, :, HD:]
-    keys[remote:, :] = own_ref[:, :HD]
-    values[remote:, :] = own_ref[:, HD:]
+        block = passage(i)
+        keys[i * PLEN : (i + 1) * PLEN, :] = block[:, :HD]
+        values[i * PLEN : (i + 1) * PLEN, :] = block[:, HD:]
+    keys[remote:, :] = own_ref[rows, :HD]
+    values[remote:, :] = own_ref[rows, HD:]
     row = lax.broadcasted_iota(jnp.int32, (2 * tokens, tokens), 0)
     col = lax.broadcasted_iota(jnp.int32, (2 * tokens, tokens), 1)
     hidden = col > jnp.where(row >= tokens, row - tokens, row)
@@ -527,8 +518,8 @@
 
     for pair in range(group // 2):
         lo, mid, hi = 2 * pair * HD, (2 * pair + 1) * HD, (2 * pair + 2) * HD
-        q = jnp.concatenate([q_ref[:, lo:mid], q_ref[:, mid:hi]], axis=0)
-        g = jnp.concatenate([g_ref[:, lo:mid], g_ref[:, mid:hi]], axis=0)
+        q = jnp.concatenate([q_ref[rows, lo:mid], q_ref[rows, mid:hi]], axis=0)
+        g = jnp.concatenate([g_ref[rows, lo:mid], g_ref[rows, mid:hi]], axis=0)
         k, v = keys[...], values[...]
         scores = dot(q, k, ((1,), (1,)))
         tail = jnp.where(hidden, jnp.float32(-1e30), scores[:, remote:])
@@ -541,8 +532,8 @@
         delta = jnp.sum(outputs * g.astype(jnp.float32), axis=1, keepdims=True)
         grad = (weights * (dot(g, v, ((1,), (1,))) - delta)).astype(jnp.bfloat16)
         dq = (dot(grad, k, ((1,), (0,))) * scaling).astype(dq_ref.dtype)
-        dq_ref[:, lo:mid] = dq[:tokens]
-        dq_ref[:, mid:hi] = dq[tokens:]
+        dq_ref[rows, lo:mid] = dq[:tokens]
+        dq_ref[rows, mid:hi] = dq[tokens:]
         dk = dot(grad, q, ((0,), (0,)))
         dv = dot(low, g, ((0,), (0,)))
         if pair == 0:
@@ -551,17 +542,231 @@
         else:
             dkeys[...] += dk
             dvalues[...] += dv
-    for i in range(retrieved):
+        between(pair)
+
+
+def grad_rows(rows, dkeys, dvalues):
+    scaling = HD ** (-0.5)
+    both = jnp.concatenate([dkeys[rows, :] * scaling, dvalues[rows, :]], axis=1)
+    return both.astype(jnp.bfloat16)
+
+
+def early_kernel(
+    chips, group, retrieved, ids_ref, x_ref, q_ref, g_ref, own_ref,
+    late_ref, dq_ref, remote_ref, down_ref, early, keys, values, dkeys, dvalues,
+    own_sem, ring_send, ring_recv, pair_send, pair_recv,
+):
+    core, place, chip_at = ring_place(chips)
+    mine = chip_at(place)
+    partner = 2 * mine + 1 - core
+    nexts = (2 * chip_at(place + 1) + core, 2 * chip_at(place - 1) + core)
+    here = x_ref.shape[0]
+    per = here // 4
+    wide = 2 * HD
+    remote = retrieved * PLEN
+    tokens = keys.shape[0] - remote
+    targets = (early, late_ref)
+
+    def first(step, way, lane, side):
+        where = chip_at(place - step if way == 0 else place + step)
+        return (2 * where + side) * here + (2 * way + lane) * per
+
+    def block(head, step, way, lane):
+        return targets[head].at[pl.ds(first(step, way, lane, core), per)]
+
+    def source(head, way, lane):
+        return x_ref.at[pl.ds((2 * way + lane) * per, per), :, pl.ds(head * wide, wide)]
+
+    def ring_copy(head, step, way, lane, src):
+        return send(
+            src, block(head, step, way, lane),
+            ring_send.at[head, step, way, lane], ring_recv.at[head, step, way, lane], nexts[way],
+        )
+
+    def pair_copy(head, step, way, lane, src):
+        return send(
+            src, block(head, step, way, lane),
+            pair_send.at[head, step, way, lane], pair_recv.at[head, step, way, lane], partner,
+        )
+
+    def own_copy(head):
+        return pltpu.make_async_copy(
+            x_ref.at[:, :, pl.ds(head * wide, wide)],
+            targets[head].at[pl.ds((2 * mine + core) * here, here)],
+            own_sem.at[head],
+        )
+
+    def begin(head):
+        for lane in range(2):
+            for way in range(2):
+                ring_copy(head, 0, way, lane, source(head, way, lane)).start()
+                pair_copy(head, 0, way, lane, source(head, way, lane)).start()
+        own_copy(head).start()
+
+    def serve(head, step):
+        for lane in range(2):
+            for way in range(2):
+                slot = block(head, step, way, lane)
+                ring_copy(head, step - 1, way, lane, slot).wait_recv()
+
+                @pl.when(step < chips - 1)
+                def _(way=way, lane=lane, slot=slot):
+                    ring_copy(head, step, way, lane, slot).start()
+
+                pair_copy(head, step, way, lane, slot).start()
+
+    def finish_pairs(head):
+        def one(step, carry):
+            for lane in range(2):
+                for way in range(2):
+                    pair_copy(head, step, way, lane, block(head, step, way, lane)).wait_recv()
+            return carry
+
+        lax.fori_loop(0, chips, one, 0)
+        own_copy(head).wait()
+
+    greet((nexts[0], nexts[1], partner))
+    begin(0)
+
+    def steps(step, carry):
+        serve(0, step)
+        return carry
+
+    lax.fori_loop(1, chips - 1, steps, 0)
+    begin(1)
+    serve(0, chips - 1)
+    finish_pairs(0)
+
+    def one_query(query, carry):
+        rows = pl.ds(pl.multiple_of(query * tokens, tokens), tokens)
+
+        def between(pair):
+            if pair % 2 == 1 and pair < 4:
+                step = 2 * query + 1 + pair // 2
+
+                @pl.when(step < chips)
+                def _():
+                    serve(1, step)
+
+        attend_rows(
+            group, retrieved, rows, lambda i: early[ids_ref[query * retrieved + i]],
+            q_ref, g_ref, own_ref, dq_ref, keys, values, dkeys, dvalues, between,
+        )
+        for i in range(retrieved):
+            remote_ref[query * retrieved + i] = grad_rows(
+                slice(i * PLEN, (i + 1) * PLEN), dkeys, dvalues
+            )
+        down_ref[rows, :] = grad_rows(slice(remote, remote + tokens), dkeys, dvalues)
+        return carry
+
+    lax.fori_loop(0, q_ref.shape[0] // tokens, one_query, 0)
+    finish_pairs(1)
+
+    def sent(step, carry):
+        for head in range(2):
+            for lane in range(2):
+                for way in range(2):
+                    slot = block(head, step, way, lane)
+                    pair_copy(head, step, way, lane, slot).wait_send()
+
+                    @pl.when(step < chips - 1)
+                    def _(head=head, way=way, lane=lane, slot=slot):
+                        ring_copy(head, step, way, lane, slot).wait_send()
+
+        return carry
+
+    lax.fori_loop(0, chips, sent, 0)
+
+
+def early_attend(ids, queries, out_grad, query_kv, projected, chips, queries_here, retrieved, collective_id):
+    rows, _ = projected.shape
+    here = rows // PLEN
+    total = 2 * chips * here
+    wide = 2 * HD
+    heads = query_kv.shape[1] // wide
+    broad = queries.shape[1] // heads
+    tokens = queries.shape[0] // queries_here
+    keys = retrieved * PLEN + tokens
+    sems = pltpu.SemaphoreType.DMA((2, chips, 2, 2))
+    return pl.pallas_call(
+        functools.partial(early_kernel, chips, broad // HD, retrieved),
+        grid=(1,),
+        out_shape=[
+            jax.ShapeDtypeStruct((total, PLEN, wide), jnp.bfloat16),
+            jax.ShapeDtypeStruct((queries.shape[0], broad), jnp.bfloat16),
+            jax.ShapeDtypeStruct((queries_here * retrieved, PLEN, wide), jnp.bfloat16),
+            jax.ShapeDtypeStruct((queries.shape[0], wide), jnp.bfloat16),
+        ],
+        in_specs=[
+            pl.BlockSpec(memory_space=pltpu.SMEM),
+            pl.BlockSpec(memory_space=pl.ANY),
+            pl.BlockSpec((queries.shape[0], broad), lambda i: (0, 0)),
+            pl.BlockSpec((queries.shape[0], broad), lambda i: (0, 0)),
+            pl.BlockSpec((queries.shape[0], wide), lambda i: (0, 0)),
+        ],
+        out_specs=[
+            pl.BlockSpec(memory_space=pl.ANY),
+            pl.BlockSpec((queries.shape[0], broad), lambda i: (0, 0)),
+            pl.BlockSpec((queries_here * retrieved, PLEN, wide), lambda i: (0, 0, 0)),
+            pl.BlockSpec((queries.shape[0], wide), lambda i: (0, 0)),
+        ],
+        scratch_shapes=[
+            pltpu.VMEM((total, PLEN, wide), jnp.bfloat16),
+            pltpu.VMEM((keys, HD), jnp.bfloat16),
+            pltpu.VMEM((keys, HD), jnp.bfloat16),
+            pltpu.VMEM((keys, HD), jnp.float32),
+            pltpu.VMEM((keys, HD), jnp.float32),
+            pltpu.SemaphoreType.DMA((2,)),
+            sems, sems, sems, sems,
+        ],
+        compiler_params=pltpu.CompilerParams(
+            collective_id=collective_id, has_side_effects=True, vmem_limit_bytes=56 * MIB
+        ),
+    )(ids, projected.reshape(here, PLEN, -1), queries, out_grad, query_kv)
+
+
+def attend_kernel(group, retrieved, ready, ids_ref, q_ref, g_ref, own_ref, *refs):
+    done, refs = refs[: 3 * ready], refs[3 * ready :]
+    passages = refs[:retrieved]
+    dq_ref, dense_ref, down_ref, keys, values, dkeys, dvalues = refs[retrieved:]
+    remote = retrieved * PLEN
+    tokens = q_ref.shape[0]
+    head, query = pl.program_id(0), pl.program_id(1)
+
+    @pl.when(query == 0)
+    def _():
+        def clear(p, carry):
+            dense_ref[p] = jnp.zeros(dense_ref.shape[1:], dense_ref.dtype)
+            return carry
+
+        lax.fori_loop(0, dense_ref.shape[0], clear, 0)
+
+    def place(i, block):
         p = ids_ref[query * retrieved + i]
-        rows = slice(i * PLEN, (i + 1) * PLEN)
-        pair = jnp.concatenate([dkeys[rows, :] * scaling, dvalues[rows, :]], axis=1)
-        pair = pair.astype(jnp.bfloat16).astype(jnp.float32)
-        dense_ref[p] = (dense_ref[p].astype(jnp.float32) + pair).astype(dense_ref.dtype)
-    down_ref[:, :HD] = (dkeys[remote:, :] * scaling).astype(down_ref.dtype)
-    down_ref[:, HD:] = dvalues[remote:, :].astype(down_ref.dtype)
-
-
-def attend(ids, queries, out_grad, query_kv, passage_kv, queries_here, retrieved):
+        total = dense_ref[p].astype(jnp.float32) + block.astype(jnp.float32)
+        dense_ref[p] = total.astype(dense_ref.dtype)
+
+    if ready:
+
+        @pl.when(head == 0)
+        def _():
+            for i in range(retrieved):
+                place(i, done[1][i])
+            dq_ref[...] = done[0][...]
+            down_ref[...] = done[2][...]
+
+    @pl.when(head >= ready)
+    def _():
+        attend_rows(
+            group, retrieved, slice(0, tokens), lambda i: passages[i][0],
+            q_ref, g_ref, own_ref, dq_ref, keys, values, dkeys, dvalues, lambda pair: None,
+        )
+        for i in range(retrieved):
+            place(i, grad_rows(slice(i * PLEN, (i + 1) * PLEN), dkeys, dvalues))
+        down_ref[...] = grad_rows(slice(remote, remote + tokens), dkeys, dvalues)
+
+
+def attend(ids, queries, out_grad, query_kv, passage_kv, queries_here, retrieved, done=()):
     tokens = queries.shape[0] // queries_here
     width = query_kv.shape[1]
     heads = width // (2 * HD)
@@ -569,18 +774,33 @@
     group = wide // HD
     keys = retrieved * PLEN + tokens
 
+    ready = 1 if done else 0
+
     def passage_spec(i):
-        return pl.BlockSpec((1, PLEN, 2 * HD), lambda h, n, ids: (ids[n * retrieved + i], 0, h))
-
+        def where(h, n, ids):
+            if ready:
+                return ids[n * h * retrieved + i], 0, 0
+            return ids[n * retrieved + i], 0, h
+
+        return pl.BlockSpec((1, PLEN, 2 * HD), where)
+
+    def done_row(h, n):
+        return n * (1 - h) + (queries_here - 1) * h
+
+    done_specs = [
+        pl.BlockSpec((tokens, wide), lambda h, n, ids: (done_row(h, n), 0)),
+        pl.BlockSpec((retrieved, PLEN, 2 * HD), lambda h, n, ids: (done_row(h, n), 0, 0)),
+        pl.BlockSpec((tokens, 2 * HD), lambda h, n, ids: (done_row(h, n), 0)),
+    ][: len(done)]
     wide_spec = pl.BlockSpec((tokens, wide), lambda h, n, ids: (n, h))
     own_spec = pl.BlockSpec((tokens, 2 * HD), lambda h, n, ids: (n, h))
     flops = 12 * queries_here * heads * group * tokens * keys * HD
     return pl.pallas_call(
-        functools.partial(attend_kernel, group, retrieved),
+        functools.partial(attend_kernel, group, retrieved, ready),
         grid_spec=pltpu.PrefetchScalarGridSpec(
             num_scalar_prefetch=1,
             grid=(heads, queries_here),
-            in_specs=[wide_spec, wide_spec, own_spec] + [passage_spec(i) for i in range(retrieved)],
+            in_specs=[wide_spec, wide_spec, own_spec] + done_specs + [passage_spec(i) for i in range(retrieved)],
             out_specs=[
                 wide_spec,
                 pl.BlockSpec((passage_kv.shape[0], PLEN, 2 * HD), lambda h, n, ids: (0, 0, h)),
@@ -595,12 +815,12 @@
         ),
         out_shape=[
             jax.ShapeDtypeStruct(queries.shape, jnp.bfloat16),
-            jax.ShapeDtypeStruct(passage_kv.shape, jnp.bfloat16),
+            jax.ShapeDtypeStruct((passage_kv.shape[0], PLEN, width), jnp.bfloat16),
             jax.ShapeDtypeStruct(query_kv.shape, jnp.bfloat16),
         ],
         compiler_params=pltpu.CompilerParams(vmem_limit_bytes=56 * MIB),
         cost_estimate=pl.CostEstimate(flops=flops, bytes_accessed=16 * MIB, transcendentals=0),
-    )(ids, queries, out_grad, query_kv, *([passage_kv] * retrieved))
+    )(ids, queries, out_grad, query_kv, *done, *([passage_kv] * retrieved))
 
 
 def per_device(passage_hidden, kv_weight, queries, query_kv, out_grad, source_device, source_slot):
@@ -613,11 +833,17 @@
     passages_here = rows_local // PLEN
     queries_here, retrieved = source_device.shape
     projected = project(passage_hidden, kv_weight, chips, shares, 0)
-    passage_kv = ring_gather(projected, chips, 1)
-    passage_kv = passage_kv.reshape(owners * passages_here, PLEN, local_width)
     ids = (source_device * passages_here + source_slot).reshape(-1)
+    heads = local_width // (2 * HD)
+    if heads == 2 and chips <= 2 * queries_here and passages_here % 4 == 0:
+        passage_kv, *done = early_attend(
+            ids, queries, out_grad, query_kv, projected, chips, queries_here, retrieved, 1
+        )
+    else:
+        passage_kv, done = ring_gather(projected, chips, 1), ()
+        passage_kv = passage_kv.reshape(owners * passages_here, PLEN, local_width)
     grad_queries, dense, own_grads = attend(
-        ids, queries, out_grad, query_kv, passage_kv, queries_here, retrieved
+        ids, queries, out_grad, query_kv, passage_kv, queries_here, retrieved, done
     )
     dense = dense.reshape(owners * rows_local, local_width)
     weight_grad = return_grads(dense, passage_hidden, chips, shares, kv_weight.shape[0], 2)

time: 368 us -> 356 us (0.967)
  Pallas kernels: 361 us -> 349 us
    pallas_call x2, Pallas kernels: 139 us -> 129 us  [the longest x1 94.8 us: early_attend(): pl.pallas_call(functools.partial(early_kernel, chips, broad // HD, retrie...]
where the time goes in v4:
time: 356 us; the launch traced here: 355 us
  Pallas kernels  349 us (98%)
  local copies, waits for them, and re-layouts  5.15 us (1%)
    pallas_call x1, Pallas kernels, return_grads(): pl.pallas_call(functools.partial(return_kernel, chips, shares, lanes, thi...  147 us
    pallas_call x1, Pallas kernels, early_attend(): pl.pallas_call(functools.partial(early_kernel, chips, broad // HD, retrie...  94.8 us
    pallas_call x1, Pallas kernels, project(): pl.pallas_call(functools.partial(project_kernel, chips, shares, lanes), o...  72.6 us
    pallas_call x1, Pallas kernels, attend(): pl.pallas_call(functools.partial(attend_kernel, group, retrieved, ready),...  34.3 us

profile of v4, /device:TPU:0, one launch (start us, length us, event | category | flops | bytes accessed | tf_op | source)
XLA Modules:
  0.0 355.5 jit_solution(14025180245957992425)
XLA Ops:
  0.6 0.7 multiply_add_fusion
  1.3 0.6 reshape.21.ids_ref
  1.9 72.6 %shard_map.94 = bf16[4,2,2,32,1024]{4,3,2,1,0:T(8,128)(2,1)} custom-call(bf16[1024,4096]{1,0:T(8,128)(2,1)} %hidden_ref.3, bf16[2,2,16,4096]{3,2,1,0:T(8,128)(2,1)} %bitcast.11), custom_call_target="tpu_custom_call" | custom-call | tf_op jit(solution)/shard_map/pallas_call | solution.py:241
  74.6 2.3 copy.10
  76.9 94.8 %shard_map.95 = (bf16[128,128,256]{2,1,0:T(8,128)(2,1)}, bf16[512,1024]{1,0:T(8,128)(2,1)}, bf16[32,128,256]{2,1,0:T(8,128)(2,1)}, bf16[512,256]{1,0:T(8,128)(2,1)}) custom-call(s32[32]{0:T(128)} %reshape.21.ids_ref, bf16[8,128,512]{2,1,0:T(8,128)(2,1)} %bitcast.10, bf16[512,2048]{1,0:T(8,128)(2,1)} %q_ref.3, bf16[512,2048]{1,0:T(8,128)(2,1)} %g_ref.3, ...), custom_call_target="tpu_custom_call" | custom-call | tf_op jit(solution)/shard_map/pallas_call | solution.py:691
  171.7 34.3 %shard_map.96 = (bf16[512,2048]{1,0:T(8,128)(2,1)}, bf16[128,128,512]{2,1,0:T(8,128)(2,1)}, bf16[512,512]{1,0:T(8,128)(2,1)}) custom-call(s32[32]{0:T(128)} %reshape.21.ids_ref, bf16[512,2048]{1,0:T(8,128)(2,1)} %q_ref.3, bf16[512,2048]{1,0:T(8,128)(2,1)} %g_ref.3, bf16[512,512]{1,0:T(8,128)(2,1)} %own_ref.3, bf16[512,1024]{1,0:T(8,128)(2,1)} %get-tuple-element.10.refs_0_, ...), custom_call_target="tpu_custom_call" | custom-call | flops 14495514624 | bytes 16777216 | tf_op jit(solution)/shard_map/pallas_call | solution.py:798
  206.0 147.2 %shard_map.97 = f32[2,32,4096]{2,1,0:T(8,128)} custom-call(bf16[8,2,2,2,256,512]{5,4,3,2,1,0:T(8,128)(2,1)} %bitcast.7, bf16[1024,4096]{1,0:T(8,128)(2,1)} %hidden_ref.3), custom_call_target="tpu_custom_call" | custom-call | tf_op jit(solution)/shard_map/pallas_call | solution.py:475
  353.2 2.3 copy.12

commit v5 on v4

--- a/solution.py
+++ b/solution.py
@@ -461,7 +461,7 @@
     local = dense.shape[1]
     wide = 2 * HD
     heads = local // wide
-    lanes = 2
+    lanes = 4 if rows % 512 == 0 else 2
     high = rows // (2 * lanes)
     each = out_rows // 2
     thin = 2 if each % 32 == 0 else 1

time: 356 us -> 357 us (level)
  no operation moved by 1% of the time
where the time goes in v5:
time: 357 us
  Pallas kernels  350 us (98%)
  local copies, waits for them, and re-layouts  5.15 us (1%)
    pallas_call x1, Pallas kernels, return_grads(): pl.pallas_call(functools.partial(return_kernel, chips, shares, lanes, thi...  148 us
    pallas_call x1, Pallas kernels, early_attend(): pl.pallas_call(functools.partial(early_kernel, chips, broad // HD, retrie...  94.8 us
    pallas_call x1, Pallas kernels, project(): pl.pallas_call(functools.partial(project_kernel, chips, shares, lanes), o...  72.6 us
    pallas_call x1, Pallas kernels, attend(): pl.pallas_call(functools.partial(attend_kernel, group, retrieved, ready),...  34.3 us

profile of v5, /device:TPU:0, one launch (start us, length us, event | category | flops | bytes accessed | tf_op | source)
XLA Modules:
  0.0 356.6 jit_solution(16754917225346748824)
XLA Ops:
  0.6 0.7 multiply_add_fusion
  1.3 0.6 reshape.21.ids_ref
  1.9 72.6 %shard_map.94 = bf16[4,2,2,32,1024]{4,3,2,1,0:T(8,128)(2,1)} custom-call(bf16[1024,4096]{1,0:T(8,128)(2,1)} %hidden_ref.3, bf16[2,2,16,4096]{3,2,1,0:T(8,128)(2,1)} %bitcast.11), custom_call_target="tpu_custom_call" | custom-call | tf_op jit(solution)/shard_map/pallas_call | solution.py:241
  74.6 2.3 copy.10
  76.9 94.8 %shard_map.95 = (bf16[128,128,256]{2,1,0:T(8,128)(2,1)}, bf16[512,1024]{1,0:T(8,128)(2,1)}, bf16[32,128,256]{2,1,0:T(8,128)(2,1)}, bf16[512,256]{1,0:T(8,128)(2,1)}) custom-call(s32[32]{0:T(128)} %reshape.21.ids_ref, bf16[8,128,512]{2,1,0:T(8,128)(2,1)} %bitcast.10, bf16[512,2048]{1,0:T(8,128)(2,1)} %q_ref.3, bf16[512,2048]{1,0:T(8,128)(2,1)} %g_ref.3, ...), custom_call_target="tpu_custom_call" | custom-call | tf_op jit(solution)/shard_map/pallas_call | solution.py:691
  171.7 34.3 %shard_map.96 = (bf16[512,2048]{1,0:T(8,128)(2,1)}, bf16[128,128,512]{2,1,0:T(8,128)(2,1)}, bf16[512,512]{1,0:T(8,128)(2,1)}) custom-call(s32[32]{0:T(128)} %reshape.21.ids_ref, bf16[512,2048]{1,0:T(8,128)(2,1)} %q_ref.3, bf16[512,2048]{1,0:T(8,128)(2,1)} %g_ref.3, bf16[512,512]{1,0:T(8,128)(2,1)} %own_ref.3, bf16[512,1024]{1,0:T(8,128)(2,1)} %get-tuple-element.10.refs_0_, ...), custom_call_target="tpu_custom_call" | custom-call | flops 14495514624 | bytes 16777216 | tf_op jit(solution)/shard_map/pallas_call | solution.py:798
  206.0 148.3 %shard_map.97 = f32[2,32,4096]{2,1,0:T(8,128)} custom-call(bf16[8,2,2,4,128,512]{5,4,3,2,1,0:T(8,128)(2,1)} %bitcast.7, bf16[1024,4096]{1,0:T(8,128)(2,1)} %hidden_ref.3), custom_call_target="tpu_custom_call" | custom-call | tf_op jit(solution)/shard_map/pallas_call | solution.py:475
  354.3 2.3 copy.12
